TPU v7x, 256 devices: a whole 4x4x8 slice. The times are simulated.
256 devices in a mesh: ctx: 32 (over y, x, core), tp: 8 (over z).
Axes of the slice: x: 4, y: 4, z: 8, core: 2. Of those that a mesh axis runs over, the one named last changes fastest.
Arguments:
- tokens: bfloat16 [32768, 2048], P(('ctx', 'tp')), may hold values from -6 to 6
- w_in: bfloat16 [2048, 8, 1288], P(None, 'tp'), may hold values from -0.125 to 0.125
- conv_weight: bfloat16 [4, 8, 768], P(None, 'tp'), may hold values from -3 to 3
- conv_bias: bfloat16 [8, 768], P('tp'), may hold values from -3 to 3
- dt_bias: float32 [64], P('tp'), may hold values from -3 to -1
- decay_rate: float32 [64], P('tp'), may hold values from 0 to 1, as said below
- skip_scale: float32 [64], P('tp'), may hold values from 0.5 to 1.5
- norm_gain: float32 [4096], P('tp'), may hold values from 0.1 to 1.9
- w_out: bfloat16 [4096, 2048], P('tp'), may hold values from -0.09375 to 0.09375
Outputs:
- mixed: bfloat16 [32768, 2048], P(('ctx', 'tp'))
Inputs may be any that keep to these rules, and one draw needn't show every extreme that they name: `decay_rate`: positive per-head rates.
All inputs are finite; a program needn't handle non-finite values.
Results may differ from a plain program's by a relative error of at most 0.017.
Values may be sent and summed in bfloat16 or wider, within the bound.
No kernel may reach another device: no remote copies, remote signals or barrier semaphores. Data moves between devices by JAX's collectives and lax.ppermute only.
A program may use at most 128 MiB of HBM per device.

v0:
```python
import jax
import jax.numpy as jnp
from jax import lax
from jax.sharding import PartitionSpec as P

P_SIZE = 64
N = 128
SPAN = 256


highest = lax.Precision.HIGHEST


def shifted(value, axis, steps):
    count = lax.axis_size(axis)
    first, last = (max(0, -steps), min(count, count - steps))
    return lax.ppermute(value, axis, [(source, source + steps) for source in range(first, last)])


def span_pass(state, pieces):
    span_x, span_b, span_c, span_dt, span_log = pieces
    per_group = state.shape[0] // span_b.shape[1]
    running = jnp.cumsum(span_log, axis=0)
    scores = jnp.einsum("tgn,sgn->gts", span_c, span_b, preferred_element_type=jnp.float32)
    scores = jnp.repeat(scores, per_group, axis=0)
    length = span_log.shape[0]
    lower = jnp.arange(length)[:, None] >= jnp.arange(length)[None, :]
    spread = running.T[:, :, None] - running.T[:, None, :]
    decay = jnp.exp(jnp.where(lower[None], spread, -jnp.inf))
    weights = (scores * decay * span_dt.T[:, None, :]).astype(jnp.bfloat16)
    inner = jnp.einsum("hts,shp->thp", weights, span_x, preferred_element_type=jnp.float32)
    c_heads = jnp.repeat(span_c, per_group, axis=1).astype(jnp.float32)
    carried = (
        jnp.einsum("thn,hpn->thp", c_heads, state, precision=highest) * jnp.exp(running)[:, :, None]
    )
    final_log = running[-1]
    factor = jnp.exp(final_log[None, :] - running) * span_dt
    inflow = (factor[:, :, None] * span_x).astype(jnp.bfloat16)
    b_heads = jnp.repeat(span_b, per_group, axis=1)
    added = jnp.einsum("shp,shn->hpn", inflow, b_heads, preferred_element_type=jnp.float32)
    new_state = state * jnp.exp(final_log)[:, None, None] + added
    return (new_state, inner + carried)


def run_spans(start_state, head_values, b_rows, c_rows, step_sizes, log_decay):
    number = head_values.shape[0] // SPAN

    def split(array):
        return array.reshape((number, SPAN) + array.shape[1:])

    final_state, outputs = lax.scan(
        span_pass,
        start_state,
        (split(head_values), split(b_rows), split(c_rows), split(step_sizes), split(log_decay)),
    )
    return (final_state, outputs.reshape((number * SPAN,) + outputs.shape[2:]))


def prepare(projected, rim_rows, conv_w, conv_b, bias_dt, rates, width_h, xbc_width):
    row_count = projected.shape[0]
    gate_raw = projected[:, :width_h]
    xbc_raw = projected[:, width_h : width_h + xbc_width]
    dt_raw = projected[:, width_h + xbc_width :]
    padded = jnp.concatenate([rim_rows, xbc_raw], axis=0)
    taps = conv_w.shape[0]
    summed = jnp.zeros((row_count, xbc_width), jnp.float32) + conv_b.astype(jnp.float32)[None, :]
    for tap in range(taps):
        summed = (
            summed
            + padded[tap : tap + row_count].astype(jnp.float32)
            * conv_w[tap].astype(jnp.float32)[None, :]
        )
    xbc = jax.nn.silu(summed).astype(jnp.bfloat16)
    step_sizes = jax.nn.softplus(dt_raw.astype(jnp.float32) + bias_dt[None, :])
    log_decay = -rates[None, :] * step_sizes
    return (gate_raw, xbc, step_sizes, log_decay)


def split_xbc(xbc, width_h, groups_here):
    row_count = xbc.shape[0]
    group_cols = groups_here * N
    head_values = xbc[:, :width_h].reshape(row_count, width_h // P_SIZE, P_SIZE)
    b_rows = xbc[:, width_h : width_h + group_cols].reshape(row_count, groups_here, N)
    c_rows = xbc[:, width_h + group_cols :].reshape(row_count, groups_here, N)
    return (head_values, b_rows, c_rows)


def finish(outputs, head_values, gate_raw, skip_here, gain, groups_here):
    row_count = outputs.shape[0]
    whole = outputs + skip_here[None, :, None] * head_values.astype(jnp.float32)
    gated = whole.reshape(row_count, -1) * jax.nn.silu(gate_raw.astype(jnp.float32))
    grouped = gated.reshape(row_count, groups_here, -1)
    factor = lax.rsqrt(jnp.mean(grouped * grouped, axis=2, keepdims=True) + 1e-05)
    normed = (grouped * factor).reshape(row_count, -1) * gain[None, :]
    return normed.astype(jnp.bfloat16)


def combine(earlier, later):
    return (earlier[0] + later[0], jnp.exp(later[0])[:, None, None] * earlier[1] + later[1])


def per_device(
    tokens, w_in, conv_weight, conv_bias, dt_bias, decay_rate, skip_scale, norm_gain, w_out
):
    weights = w_in.reshape(w_in.shape[0], w_in.shape[2])
    conv_w = conv_weight.reshape(conv_weight.shape[0], conv_weight.shape[2])
    conv_b = conv_bias.reshape(conv_bias.shape[1])
    width_h = norm_gain.shape[0]
    heads = decay_rate.shape[0]
    xbc_width = conv_w.shape[1]
    groups_here = (xbc_width - width_h) // (2 * N)
    per_group = heads // groups_here
    projected = jnp.dot(
        lax.all_gather(tokens, "tp", axis=0, tiled=True),
        weights,
        preferred_element_type=jnp.float32,
    ).astype(jnp.bfloat16)
    row_count = projected.shape[0]
    taps = conv_w.shape[0]
    last_rows = projected[row_count - (taps - 1) :, width_h : width_h + xbc_width]
    rim_rows = shifted(last_rows, "ctx", 1)
    gate_raw, xbc, step_sizes, log_decay = prepare(
        projected, rim_rows, conv_w, conv_b, dt_bias, decay_rate, width_h, xbc_width
    )
    head_values, b_rows, c_rows = split_xbc(xbc, width_h, groups_here)
    start_state = jnp.zeros((heads, P_SIZE, N), jnp.float32)
    local_state, local_out = run_spans(
        start_state, head_values, b_rows, c_rows, step_sizes, log_decay
    )
    block_running = jnp.cumsum(log_decay, axis=0)
    local_total = block_running[-1]
    identity = (jnp.zeros_like(local_total), jnp.zeros_like(local_state))

    def hop(turn, arriving):
        leaving = combine(arriving, (local_total, local_state))
        return shifted((leaving[0], leaving[1]), "ctx", 1)

    incoming = lax.fori_loop(0, lax.axis_size("ctx") - 1, hop, identity)
    c_float = c_rows.astype(jnp.float32)
    state_groups = incoming[1].reshape(groups_here, per_group, P_SIZE, N)
    carried = jnp.einsum("tgn,gkpn->tgkp", c_float, state_groups, precision=highest).reshape(
        row_count, heads, P_SIZE
    )
    outputs = local_out + carried * jnp.exp(block_running)[:, :, None]
    hidden = finish(outputs, head_values, gate_raw, skip_scale, norm_gain, groups_here)
    return lax.psum_scatter(
        jnp.dot(hidden, w_out, preferred_element_type=jnp.float32).astype(jnp.bfloat16),
        "tp",
        scatter_dimension=0,
        tiled=True,
    )


def solution(mesh):
    placed = (
        P(("ctx", "tp"), None),
        P(None, "tp", None),
        P(None, "tp", None),
        P("tp", None),
        P("tp"),
        P("tp"),
        P("tp"),
        P("tp"),
        P("tp", None),
    )
    return jax.shard_map(
        per_device, mesh=mesh, in_specs=placed, out_specs=P(("ctx", "tp"), None), check_vma=False
    )
```

profile of v0, /device:TPU:2, one launch (start us, length us, event | category | flops | bytes accessed | tf_op | source)
XLA Modules:
  0.0 549.1 jit_solution(12743466245632751558)
XLA Ops:
  10.4 56.6 %all-gather.2.cloned.1.call-done = bf16[1024,2048]{1,0:T(8,128)(2,1)} async-done(((bf16[128,2048]{1,0:T(8,128)(2,1)}), bf16[1024,2048]{1,0:T(8,128)(2,1)}) %all-gather.2.cloned.1.call-update) | async-done | bytes 4194320 | tf_op jit(solution)/shard_map/all_gather | solution.py:114
  66.9 9.0 %fusion.25 = bf16[1024,1288]{0,1:T(8,128)(2,1)S(1)} fusion(bf16[1024,2048]{1,0:T(8,128)(2,1)} %all-gather.2.cloned.1.call-done, bf16[2048,1,1288]{0,2,1:T(8,128)(2,1)} %param.14), kind=kOutput, calls=%fused_computation.41 | convolution fusion | flops 5403582464 | bytes 12107776 | tf_op jit(solution)/shard_map/dot_general | solution.py:113
  77.6 2.3 reduce-window.16
  80.3 2.2 collective-permute-start.1
  82.8 4.7 collective-permute-done.1
  87.5 3.5 multiply_convert_fusion.4
  94.5 2.5 copy.46
  97.4 71.4 %while.26 = (s32[]{:T(128)}, f32[8,64,128]{2,1,0:T(8,128)S(1)}, f32[4,256,8,64]{1,0,3,2:T(4,128)}, f32[4,256,8]{1,2,0:T(8,128)S(1)}, f32[4,256,8]{1,2,0:T(8,128)...) while((s32[]{:T(128)}, f32[8,64,128]{2,1,0:T(8,128)S(1)}, ...), condition=%wide.region_3.4_spmd.clone, body=%wide.region_0.3_spmd.clone.sunk | while | flops 322639904 | bytes 6316932 | solution.py:51
  100.7 1.7 fusion.72
  103.0 12.3 %dynamic_update_slice.6 = f32[4,256,8,64]{1,0,3,2:T(4,128)} dynamic-update-slice(f32[4,256,8,64]{1,0,3,2:T(4,128)} %get-tuple-element.302, f32[1,256,8,64]{1,0,3,2:T(1,128)S(1)} %copy.68, s32[]{:T(128)S(6)} %copy.73, s32[]{:T(128)} %constant.46.clone.1..sunk, s32[]{:T(128)} %constant.46.clone.1..sunk, s32[]{:T(128)} %constant.46.clone.1..sunk) | dynamic-update-slice | bytes 1048580 | tf_op jit(solution)/shard_map/while/body/jit(dynamic_update_index_in_dim)/dynamic_update_slice | solution.py:51
  118.6 1.7 fusion.72
  120.8 12.3 %dynamic_update_slice.6 = f32[4,256,8,64]{1,0,3,2:T(4,128)} dynamic-update-slice(f32[4,256,8,64]{1,0,3,2:T(4,128)} %get-tuple-element.302, f32[1,256,8,64]{1,0,3,2:T(1,128)S(1)} %copy.68, s32[]{:T(128)S(6)} %copy.73, s32[]{:T(128)} %constant.46.clone.1..sunk, s32[]{:T(128)} %constant.46.clone.1..sunk, s32[]{:T(128)} %constant.46.clone.1..sunk) | dynamic-update-slice | bytes 1048580 | tf_op jit(solution)/shard_map/while/body/jit(dynamic_update_index_in_dim)/dynamic_update_slice | solution.py:51
  136.4 1.7 fusion.72
  138.7 12.3 %dynamic_update_slice.6 = f32[4,256,8,64]{1,0,3,2:T(4,128)} dynamic-update-slice(f32[4,256,8,64]{1,0,3,2:T(4,128)} %get-tuple-element.302, f32[1,256,8,64]{1,0,3,2:T(1,128)S(1)} %copy.68, s32[]{:T(128)S(6)} %copy.73, s32[]{:T(128)} %constant.46.clone.1..sunk, s32[]{:T(128)} %constant.46.clone.1..sunk, s32[]{:T(128)} %constant.46.clone.1..sunk) | dynamic-update-slice | bytes 1048580 | tf_op jit(solution)/shard_map/while/body/jit(dynamic_update_index_in_dim)/dynamic_update_slice | solution.py:51
  156.5 12.3 %dynamic_update_slice.6 = f32[4,256,8,64]{1,0,3,2:T(4,128)} dynamic-update-slice(f32[4,256,8,64]{1,0,3,2:T(4,128)} %get-tuple-element.302, f32[1,256,8,64]{1,0,3,2:T(1,128)S(1)} %copy.68, s32[]{:T(128)S(6)} %copy.73, s32[]{:T(128)} %constant.46.clone.1..sunk, s32[]{:T(128)} %constant.46.clone.1..sunk, s32[]{:T(128)} %constant.46.clone.1..sunk) | dynamic-update-slice | bytes 1048580 | tf_op jit(solution)/shard_map/while/body/jit(dynamic_update_index_in_dim)/dynamic_update_slice | solution.py:51
  168.8 3.4 copy.61
  172.2 279.3 %while.25 = (s32[]{:T(128)}, f32[8,64,128]{2,1,0:T(8,128)S(1)}, f32[8,1,1]{0,2,1:T(1,128)S(1)}, f32[8,64,128]{2,1,0:T(8,128)S(1)}, s32[]{:T(128)}) while((s32[]{:T(128)}, f32[8,64,128]{2,1,0:T(8,128)S(1)}, f32[8,1,1]{0,2,1:T(1,128)S(1)}, f32[8,64,128]{2,1,0:T(8,128)S(1)}, s32[]{:T(128)}) %tuple.74), condition=%wide.region_7.8_spmd, body=%wide.region_6.7_spmd.sunk | while | flops 131074 | bytes 1835141 | solution.py:138
  172.3 1.9 collective-permute-start
  174.3 5.8 %collective-permute-done = f32[8,64,128]{2,1,0:T(8,128)S(1)} collective-permute-done((f32[8,64,128]{2,1,0:T(8,128)S(1)}, f32[8,64,128]{2,1,0:T(8,128)S(1)}, u32[]{:S(2)}, u32[]{:S(2)}) %collective-permute-start) | collective-permute-done | bytes 262176 | tf_op jit(solution)/shard_map/while/body/eval_jaxpr/ppermute | solution.py:17
  180.1 1.9 collective-permute-start
  182.0 5.8 %collective-permute-done = f32[8,64,128]{2,1,0:T(8,128)S(1)} collective-permute-done((f32[8,64,128]{2,1,0:T(8,128)S(1)}, f32[8,64,128]{2,1,0:T(8,128)S(1)}, u32[]{:S(2)}, u32[]{:S(2)}) %collective-permute-start) | collective-permute-done | bytes 262176 | tf_op jit(solution)/shard_map/while/body/eval_jaxpr/ppermute | solution.py:17
  187.9 1.9 collective-permute-start
  189.8 5.8 %collective-permute-done = f32[8,64,128]{2,1,0:T(8,128)S(1)} collective-permute-done((f32[8,64,128]{2,1,0:T(8,128)S(1)}, f32[8,64,128]{2,1,0:T(8,128)S(1)}, u32[]{:S(2)}, u32[]{:S(2)}) %collective-permute-start) | collective-permute-done | bytes 262176 | tf_op jit(solution)/shard_map/while/body/eval_jaxpr/ppermute | solution.py:17
  195.7 1.9 collective-permute-start
  197.6 5.8 %collective-permute-done = f32[8,64,128]{2,1,0:T(8,128)S(1)} collective-permute-done((f32[8,64,128]{2,1,0:T(8,128)S(1)}, f32[8,64,128]{2,1,0:T(8,128)S(1)}, u32[]{:S(2)}, u32[]{:S(2)}) %collective-permute-start) | collective-permute-done | bytes 262176 | tf_op jit(solution)/shard_map/while/body/eval_jaxpr/ppermute | solution.py:17
  203.5 1.9 collective-permute-start
  205.4 5.8 %collective-permute-done = f32[8,64,128]{2,1,0:T(8,128)S(1)} collective-permute-done((f32[8,64,128]{2,1,0:T(8,128)S(1)}, f32[8,64,128]{2,1,0:T(8,128)S(1)}, u32[]{:S(2)}, u32[]{:S(2)}) %collective-permute-start) | collective-permute-done | bytes 262176 | tf_op jit(solution)/shard_map/while/body/eval_jaxpr/ppermute | solution.py:17
  211.3 1.9 collective-permute-start
  213.2 5.8 %collective-permute-done = f32[8,64,128]{2,1,0:T(8,128)S(1)} collective-permute-done((f32[8,64,128]{2,1,0:T(8,128)S(1)}, f32[8,64,128]{2,1,0:T(8,128)S(1)}, u32[]{:S(2)}, u32[]{:S(2)}) %collective-permute-start) | collective-permute-done | bytes 262176 | tf_op jit(solution)/shard_map/while/body/eval_jaxpr/ppermute | solution.py:17
  219.0 1.9 collective-permute-start
  221.0 5.8 %collective-permute-done = f32[8,64,128]{2,1,0:T(8,128)S(1)} collective-permute-done((f32[8,64,128]{2,1,0:T(8,128)S(1)}, f32[8,64,128]{2,1,0:T(8,128)S(1)}, u32[]{:S(2)}, u32[]{:S(2)}) %collective-permute-start) | collective-permute-done | bytes 262176 | tf_op jit(solution)/shard_map/while/body/eval_jaxpr/ppermute | solution.py:17
  226.8 1.9 collective-permute-start
  228.8 5.8 %collective-permute-done = f32[8,64,128]{2,1,0:T(8,128)S(1)} collective-permute-done((f32[8,64,128]{2,1,0:T(8,128)S(1)}, f32[8,64,128]{2,1,0:T(8,128)S(1)}, u32[]{:S(2)}, u32[]{:S(2)}) %collective-permute-start) | collective-permute-done | bytes 262176 | tf_op jit(solution)/shard_map/while/body/eval_jaxpr/ppermute | solution.py:17
  234.6 1.9 collective-permute-start
  236.6 5.8 %collective-permute-done = f32[8,64,128]{2,1,0:T(8,128)S(1)} collective-permute-done((f32[8,64,128]{2,1,0:T(8,128)S(1)}, f32[8,64,128]{2,1,0:T(8,128)S(1)}, u32[]{:S(2)}, u32[]{:S(2)}) %collective-permute-start) | collective-permute-done | bytes 262176 | tf_op jit(solution)/shard_map/while/body/eval_jaxpr/ppermute | solution.py:17
  242.4 1.9 collective-permute-start
  244.3 5.8 %collective-permute-done = f32[8,64,128]{2,1,0:T(8,128)S(1)} collective-permute-done((f32[8,64,128]{2,1,0:T(8,128)S(1)}, f32[8,64,128]{2,1,0:T(8,128)S(1)}, u32[]{:S(2)}, u32[]{:S(2)}) %collective-permute-start) | collective-permute-done | bytes 262176 | tf_op jit(solution)/shard_map/while/body/eval_jaxpr/ppermute | solution.py:17
  250.2 2.3 collective-permute-start
  252.5 5.4 collective-permute-done
  258.0 4.4 collective-permute-start
  262.4 3.3 collective-permute-done
  265.8 6.5 %collective-permute-start = (f32[8,64,128]{2,1,0:T(8,128)S(1)}, f32[8,64,128]{2,1,0:T(8,128)S(1)}, u32[]{:S(2)}, u32[]{:S(2)}) collective-permute-start(f32[8,64,128]{2,1,0:T(8,128)S(1)} %multiply_add_fusion.2), channel_id=1, source_target_pairs={{0,8},{8,16},{16,24},{24,32},{32,40},{40,48},{48,56},{56,64},{64,7... | collective-permute-start | bytes 786440 | tf_op jit(solution)/shard_map/while/body/eval_jaxpr/ppermute | solution.py:17
  273.5 8.6 %collective-permute-start = (f32[8,64,128]{2,1,0:T(8,128)S(1)}, f32[8,64,128]{2,1,0:T(8,128)S(1)}, u32[]{:S(2)}, u32[]{:S(2)}) collective-permute-start(f32[8,64,128]{2,1,0:T(8,128)S(1)} %multiply_add_fusion.2), channel_id=1, source_target_pairs={{0,8},{8,16},{16,24},{24,32},{32,40},{40,48},{48,56},{56,64},{64,7... | collective-permute-start | bytes 786440 | tf_op jit(solution)/shard_map/while/body/eval_jaxpr/ppermute | solution.py:17
  283.4 8.7 %collective-permute-start = (f32[8,64,128]{2,1,0:T(8,128)S(1)}, f32[8,64,128]{2,1,0:T(8,128)S(1)}, u32[]{:S(2)}, u32[]{:S(2)}) collective-permute-start(f32[8,64,128]{2,1,0:T(8,128)S(1)} %multiply_add_fusion.2), channel_id=1, source_target_pairs={{0,8},{8,16},{16,24},{24,32},{32,40},{40,48},{48,56},{56,64},{64,7... | collective-permute-start | bytes 786440 | tf_op jit(solution)/shard_map/while/body/eval_jaxpr/ppermute | solution.py:17
  293.3 8.7 %collective-permute-start = (f32[8,64,128]{2,1,0:T(8,128)S(1)}, f32[8,64,128]{2,1,0:T(8,128)S(1)}, u32[]{:S(2)}, u32[]{:S(2)}) collective-permute-start(f32[8,64,128]{2,1,0:T(8,128)S(1)} %multiply_add_fusion.2), channel_id=1, source_target_pairs={{0,8},{8,16},{16,24},{24,32},{32,40},{40,48},{48,56},{56,64},{64,7... | collective-permute-start | bytes 786440 | tf_op jit(solution)/shard_map/while/body/eval_jaxpr/ppermute | solution.py:17
  303.2 8.7 %collective-permute-start = (f32[8,64,128]{2,1,0:T(8,128)S(1)}, f32[8,64,128]{2,1,0:T(8,128)S(1)}, u32[]{:S(2)}, u32[]{:S(2)}) collective-permute-start(f32[8,64,128]{2,1,0:T(8,128)S(1)} %multiply_add_fusion.2), channel_id=1, source_target_pairs={{0,8},{8,16},{16,24},{24,32},{32,40},{40,48},{48,56},{56,64},{64,7... | collective-permute-start | bytes 786440 | tf_op jit(solution)/shard_map/while/body/eval_jaxpr/ppermute | solution.py:17
  313.1 8.7 %collective-permute-start = (f32[8,64,128]{2,1,0:T(8,128)S(1)}, f32[8,64,128]{2,1,0:T(8,128)S(1)}, u32[]{:S(2)}, u32[]{:S(2)}) collective-permute-start(f32[8,64,128]{2,1,0:T(8,128)S(1)} %multiply_add_fusion.2), channel_id=1, source_target_pairs={{0,8},{8,16},{16,24},{24,32},{32,40},{40,48},{48,56},{56,64},{64,7... | collective-permute-start | bytes 786440 | tf_op jit(solution)/shard_map/while/body/eval_jaxpr/ppermute | solution.py:17
  323.0 8.7 %collective-permute-start = (f32[8,64,128]{2,1,0:T(8,128)S(1)}, f32[8,64,128]{2,1,0:T(8,128)S(1)}, u32[]{:S(2)}, u32[]{:S(2)}) collective-permute-start(f32[8,64,128]{2,1,0:T(8,128)S(1)} %multiply_add_fusion.2), channel_id=1, source_target_pairs={{0,8},{8,16},{16,24},{24,32},{32,40},{40,48},{48,56},{56,64},{64,7... | collective-permute-start | bytes 786440 | tf_op jit(solution)/shard_map/while/body/eval_jaxpr/ppermute | solution.py:17
  332.9 8.7 %collective-permute-start = (f32[8,64,128]{2,1,0:T(8,128)S(1)}, f32[8,64,128]{2,1,0:T(8,128)S(1)}, u32[]{:S(2)}, u32[]{:S(2)}) collective-permute-start(f32[8,64,128]{2,1,0:T(8,128)S(1)} %multiply_add_fusion.2), channel_id=1, source_target_pairs={{0,8},{8,16},{16,24},{24,32},{32,40},{40,48},{48,56},{56,64},{64,7... | collective-permute-start | bytes 786440 | tf_op jit(solution)/shard_map/while/body/eval_jaxpr/ppermute | solution.py:17
  342.8 8.7 %collective-permute-start = (f32[8,64,128]{2,1,0:T(8,128)S(1)}, f32[8,64,128]{2,1,0:T(8,128)S(1)}, u32[]{:S(2)}, u32[]{:S(2)}) collective-permute-start(f32[8,64,128]{2,1,0:T(8,128)S(1)} %multiply_add_fusion.2), channel_id=1, source_target_pairs={{0,8},{8,16},{16,24},{24,32},{32,40},{40,48},{48,56},{56,64},{64,7... | collective-permute-start | bytes 786440 | tf_op jit(solution)/shard_map/while/body/eval_jaxpr/ppermute | solution.py:17
  352.7 8.7 %collective-permute-start = (f32[8,64,128]{2,1,0:T(8,128)S(1)}, f32[8,64,128]{2,1,0:T(8,128)S(1)}, u32[]{:S(2)}, u32[]{:S(2)}) collective-permute-start(f32[8,64,128]{2,1,0:T(8,128)S(1)} %multiply_add_fusion.2), channel_id=1, source_target_pairs={{0,8},{8,16},{16,24},{24,32},{32,40},{40,48},{48,56},{56,64},{64,7... | collective-permute-start | bytes 786440 | tf_op jit(solution)/shard_map/while/body/eval_jaxpr/ppermute | solution.py:17
  362.6 8.7 %collective-permute-start = (f32[8,64,128]{2,1,0:T(8,128)S(1)}, f32[8,64,128]{2,1,0:T(8,128)S(1)}, u32[]{:S(2)}, u32[]{:S(2)}) collective-permute-start(f32[8,64,128]{2,1,0:T(8,128)S(1)} %multiply_add_fusion.2), channel_id=1, source_target_pairs={{0,8},{8,16},{16,24},{24,32},{32,40},{40,48},{48,56},{56,64},{64,7... | collective-permute-start | bytes 786440 | tf_op jit(solution)/shard_map/while/body/eval_jaxpr/ppermute | solution.py:17
  372.5 8.7 %collective-permute-start = (f32[8,64,128]{2,1,0:T(8,128)S(1)}, f32[8,64,128]{2,1,0:T(8,128)S(1)}, u32[]{:S(2)}, u32[]{:S(2)}) collective-permute-start(f32[8,64,128]{2,1,0:T(8,128)S(1)} %multiply_add_fusion.2), channel_id=1, source_target_pairs={{0,8},{8,16},{16,24},{24,32},{32,40},{40,48},{48,56},{56,64},{64,7... | collective-permute-start | bytes 786440 | tf_op jit(solution)/shard_map/while/body/eval_jaxpr/ppermute | solution.py:17
  382.4 8.7 %collective-permute-start = (f32[8,64,128]{2,1,0:T(8,128)S(1)}, f32[8,64,128]{2,1,0:T(8,128)S(1)}, u32[]{:S(2)}, u32[]{:S(2)}) collective-permute-start(f32[8,64,128]{2,1,0:T(8,128)S(1)} %multiply_add_fusion.2), channel_id=1, source_target_pairs={{0,8},{8,16},{16,24},{24,32},{32,40},{40,48},{48,56},{56,64},{64,7... | collective-permute-start | bytes 786440 | tf_op jit(solution)/shard_map/while/body/eval_jaxpr/ppermute | solution.py:17
  392.3 8.7 %collective-permute-start = (f32[8,64,128]{2,1,0:T(8,128)S(1)}, f32[8,64,128]{2,1,0:T(8,128)S(1)}, u32[]{:S(2)}, u32[]{:S(2)}) collective-permute-start(f32[8,64,128]{2,1,0:T(8,128)S(1)} %multiply_add_fusion.2), channel_id=1, source_target_pairs={{0,8},{8,16},{16,24},{24,32},{32,40},{40,48},{48,56},{56,64},{64,7... | collective-permute-start | bytes 786440 | tf_op jit(solution)/shard_map/while/body/eval_jaxpr/ppermute | solution.py:17
  402.2 8.7 %collective-permute-start = (f32[8,64,128]{2,1,0:T(8,128)S(1)}, f32[8,64,128]{2,1,0:T(8,128)S(1)}, u32[]{:S(2)}, u32[]{:S(2)}) collective-permute-start(f32[8,64,128]{2,1,0:T(8,128)S(1)} %multiply_add_fusion.2), channel_id=1, source_target_pairs={{0,8},{8,16},{16,24},{24,32},{32,40},{40,48},{48,56},{56,64},{64,7... | collective-permute-start | bytes 786440 | tf_op jit(solution)/shard_map/while/body/eval_jaxpr/ppermute | solution.py:17
  412.1 8.7 %collective-permute-start = (f32[8,64,128]{2,1,0:T(8,128)S(1)}, f32[8,64,128]{2,1,0:T(8,128)S(1)}, u32[]{:S(2)}, u32[]{:S(2)}) collective-permute-start(f32[8,64,128]{2,1,0:T(8,128)S(1)} %multiply_add_fusion.2), channel_id=1, source_target_pairs={{0,8},{8,16},{16,24},{24,32},{32,40},{40,48},{48,56},{56,64},{64,7... | collective-permute-start | bytes 786440 | tf_op jit(solution)/shard_map/while/body/eval_jaxpr/ppermute | solution.py:17
  422.0 8.7 %collective-permute-start = (f32[8,64,128]{2,1,0:T(8,128)S(1)}, f32[8,64,128]{2,1,0:T(8,128)S(1)}, u32[]{:S(2)}, u32[]{:S(2)}) collective-permute-start(f32[8,64,128]{2,1,0:T(8,128)S(1)} %multiply_add_fusion.2), channel_id=1, source_target_pairs={{0,8},{8,16},{16,24},{24,32},{32,40},{40,48},{48,56},{56,64},{64,7... | collective-permute-start | bytes 786440 | tf_op jit(solution)/shard_map/while/body/eval_jaxpr/ppermute | solution.py:17
  431.9 8.7 %collective-permute-start = (f32[8,64,128]{2,1,0:T(8,128)S(1)}, f32[8,64,128]{2,1,0:T(8,128)S(1)}, u32[]{:S(2)}, u32[]{:S(2)}) collective-permute-start(f32[8,64,128]{2,1,0:T(8,128)S(1)} %multiply_add_fusion.2), channel_id=1, source_target_pairs={{0,8},{8,16},{16,24},{24,32},{32,40},{40,48},{48,56},{56,64},{64,7... | collective-permute-start | bytes 786440 | tf_op jit(solution)/shard_map/while/body/eval_jaxpr/ppermute | solution.py:17
  441.8 8.7 %collective-permute-start = (f32[8,64,128]{2,1,0:T(8,128)S(1)}, f32[8,64,128]{2,1,0:T(8,128)S(1)}, u32[]{:S(2)}, u32[]{:S(2)}) collective-permute-start(f32[8,64,128]{2,1,0:T(8,128)S(1)} %multiply_add_fusion.2), channel_id=1, source_target_pairs={{0,8},{8,16},{16,24},{24,32},{32,40},{40,48},{48,56},{56,64},{64,7... | collective-permute-start | bytes 786440 | tf_op jit(solution)/shard_map/while/body/eval_jaxpr/ppermute | solution.py:17
  451.6 2.0 fusion.38
  453.6 3.0 multiply_reduce_fusion
  456.7 4.4 convolution_convert_fusion
  461.1 81.2 %reduce-scatter.2.cloned.1.call-done = bf16[128,2048]{1,0:T(8,128)(2,1)} async-done(((bf16[1024,2048]{1,0:T(8,128)(2,1)}), bf16[128,2048]{1,0:T(8,128)(2,1)}) %reduce-scatter.2.cloned.1.call-update) | async-done | bytes 524304 | tf_op jit(solution)/shard_map/reduce_scatter | solution.py:146
  (164 shorter events, 51.3 us)
Async XLA Ops:
  6.5 450.1 %copy-start = (bf16[512,2048]{1,0:T(8,128)(2,1)S(1)}, bf16[512,2048]{1,0:T(8,128)(2,1)}, u32[]{:S(2)}) copy-start(bf16[512,2048]{1,0:T(8,128)(2,1)} %param.21) | copy-start | bytes 6291460
  6.5 60.4 %all-gather.2.cloned.1.call-start = ((), (), s32[]{:S(2)}) async-start(), calls=%async_computation.1 | async-start | bytes 4718592 | tf_op jit(solution)/shard_map/all_gather | solution.py:114
  7.3 535.0 %reduce-scatter.2.cloned.1.call-start = ((), (), s32[]{:S(2)}) async-start(), calls=%async_computation.2 | async-start | bytes 4718592 | tf_op jit(solution)/shard_map/reduce_scatter | solution.py:146
  10.4 67.1 %copy-start.6 = (f32[8]{0:T(128)S(1)}, f32[8]{0:T(128)}, u32[]{:S(2)}) copy-start(f32[8]{0:T(128)} %param.17) | copy-start | bytes 100
  76.0 1.5 copy-start.3
  80.2 7.2 %slice-start = ((bf16[1024,1288]{0,1:T(8,128)(2,1)}), bf16[1024,768]{0,1:T(8,128)(2,1)S(1)}, s32[]{:S(2)}) async-start(bf16[1024,1288]{0,1:T(8,128)(2,1)} %copy-done.3), calls=%async_computation.3 | async-start | bytes 3145728 | tf_op jit(solution)/shard_map/slice | solution.py:62
  80.3 7.1 %collective-permute-start.1 = (bf16[3,768]{0,1:T(8,128)(2,1)S(1)}, bf16[3,768]{0,1:T(8,128)(2,1)S(1)}, u32[]{:S(2)}, u32[]{:S(2)}) collective-permute-start(bf16[3,768]{0,1:T(8,128)(2,1)S(1)} %slice.87), channel_id=1, source_target_pairs={{0,8},{8,16},{16,24},{24,32},{32,40},{40,48},{48,56},{56,64},{64,7... | collective-permute-start | bytes 13832 | tf_op jit(solution)/shard_map/ppermute | solution.py:17
  91.0 1.1 copy-start.1
  94.5 2.5 copy-start.5
  94.5 2.7 copy-start.4
  172.3 7.7 %collective-permute-start = (f32[8,64,128]{2,1,0:T(8,128)S(1)}, f32[8,64,128]{2,1,0:T(8,128)S(1)}, u32[]{:S(2)}, u32[]{:S(2)}) collective-permute-start(f32[8,64,128]{2,1,0:T(8,128)S(1)} %multiply_add_fusion.2), channel_id=1, source_target_pairs={{0,8},{8,16},{16,24},{24,32},{32,40},{40,48},{48,56},{56,64},{64,7... | collective-permute-start | bytes 786440 | tf_op jit(solution)/shard_map/while/body/eval_jaxpr/ppermute | solution.py:17
  180.1 7.7 %collective-permute-start = (f32[8,64,128]{2,1,0:T(8,128)S(1)}, f32[8,64,128]{2,1,0:T(8,128)S(1)}, u32[]{:S(2)}, u32[]{:S(2)}) collective-permute-start(f32[8,64,128]{2,1,0:T(8,128)S(1)} %multiply_add_fusion.2), channel_id=1, source_target_pairs={{0,8},{8,16},{16,24},{24,32},{32,40},{40,48},{48,56},{56,64},{64,7... | collective-permute-start | bytes 786440 | tf_op jit(solution)/shard_map/while/body/eval_jaxpr/ppermute | solution.py:17
  187.9 7.7 %collective-permute-start = (f32[8,64,128]{2,1,0:T(8,128)S(1)}, f32[8,64,128]{2,1,0:T(8,128)S(1)}, u32[]{:S(2)}, u32[]{:S(2)}) collective-permute-start(f32[8,64,128]{2,1,0:T(8,128)S(1)} %multiply_add_fusion.2), channel_id=1, source_target_pairs={{0,8},{8,16},{16,24},{24,32},{32,40},{40,48},{48,56},{56,64},{64,7... | collective-permute-start | bytes 786440 | tf_op jit(solution)/shard_map/while/body/eval_jaxpr/ppermute | solution.py:17
  195.7 7.7 %collective-permute-start = (f32[8,64,128]{2,1,0:T(8,128)S(1)}, f32[8,64,128]{2,1,0:T(8,128)S(1)}, u32[]{:S(2)}, u32[]{:S(2)}) collective-permute-start(f32[8,64,128]{2,1,0:T(8,128)S(1)} %multiply_add_fusion.2), channel_id=1, source_target_pairs={{0,8},{8,16},{16,24},{24,32},{32,40},{40,48},{48,56},{56,64},{64,7... | collective-permute-start | bytes 786440 | tf_op jit(solution)/shard_map/while/body/eval_jaxpr/ppermute | solution.py:17
  203.5 7.7 %collective-permute-start = (f32[8,64,128]{2,1,0:T(8,128)S(1)}, f32[8,64,128]{2,1,0:T(8,128)S(1)}, u32[]{:S(2)}, u32[]{:S(2)}) collective-permute-start(f32[8,64,128]{2,1,0:T(8,128)S(1)} %multiply_add_fusion.2), channel_id=1, source_target_pairs={{0,8},{8,16},{16,24},{24,32},{32,40},{40,48},{48,56},{56,64},{64,7... | collective-permute-start | bytes 786440 | tf_op jit(solution)/shard_map/while/body/eval_jaxpr/ppermute | solution.py:17
  211.3 7.7 %collective-permute-start = (f32[8,64,128]{2,1,0:T(8,128)S(1)}, f32[8,64,128]{2,1,0:T(8,128)S(1)}, u32[]{:S(2)}, u32[]{:S(2)}) collective-permute-start(f32[8,64,128]{2,1,0:T(8,128)S(1)} %multiply_add_fusion.2), channel_id=1, source_target_pairs={{0,8},{8,16},{16,24},{24,32},{32,40},{40,48},{48,56},{56,64},{64,7... | collective-permute-start | bytes 786440 | tf_op jit(solution)/shard_map/while/body/eval_jaxpr/ppermute | solution.py:17
  219.0 7.7 %collective-permute-start = (f32[8,64,128]{2,1,0:T(8,128)S(1)}, f32[8,64,128]{2,1,0:T(8,128)S(1)}, u32[]{:S(2)}, u32[]{:S(2)}) collective-permute-start(f32[8,64,128]{2,1,0:T(8,128)S(1)} %multiply_add_fusion.2), channel_id=1, source_target_pairs={{0,8},{8,16},{16,24},{24,32},{32,40},{40,48},{48,56},{56,64},{64,7... | collective-permute-start | bytes 786440 | tf_op jit(solution)/shard_map/while/body/eval_jaxpr/ppermute | solution.py:17
  226.8 7.7 %collective-permute-start = (f32[8,64,128]{2,1,0:T(8,128)S(1)}, f32[8,64,128]{2,1,0:T(8,128)S(1)}, u32[]{:S(2)}, u32[]{:S(2)}) collective-permute-start(f32[8,64,128]{2,1,0:T(8,128)S(1)} %multiply_add_fusion.2), channel_id=1, source_target_pairs={{0,8},{8,16},{16,24},{24,32},{32,40},{40,48},{48,56},{56,64},{64,7... | collective-permute-start | bytes 786440 | tf_op jit(solution)/shard_map/while/body/eval_jaxpr/ppermute | solution.py:17
  234.6 7.7 %collective-permute-start = (f32[8,64,128]{2,1,0:T(8,128)S(1)}, f32[8,64,128]{2,1,0:T(8,128)S(1)}, u32[]{:S(2)}, u32[]{:S(2)}) collective-permute-start(f32[8,64,128]{2,1,0:T(8,128)S(1)} %multiply_add_fusion.2), channel_id=1, source_target_pairs={{0,8},{8,16},{16,24},{24,32},{32,40},{40,48},{48,56},{56,64},{64,7... | collective-permute-start | bytes 786440 | tf_op jit(solution)/shard_map/while/body/eval_jaxpr/ppermute | solution.py:17
  242.4 7.7 %collective-permute-start = (f32[8,64,128]{2,1,0:T(8,128)S(1)}, f32[8,64,128]{2,1,0:T(8,128)S(1)}, u32[]{:S(2)}, u32[]{:S(2)}) collective-permute-start(f32[8,64,128]{2,1,0:T(8,128)S(1)} %multiply_add_fusion.2), channel_id=1, source_target_pairs={{0,8},{8,16},{16,24},{24,32},{32,40},{40,48},{48,56},{56,64},{64,7... | collective-permute-start | bytes 786440 | tf_op jit(solution)/shard_map/while/body/eval_jaxpr/ppermute | solution.py:17
  250.2 7.7 %collective-permute-start = (f32[8,64,128]{2,1,0:T(8,128)S(1)}, f32[8,64,128]{2,1,0:T(8,128)S(1)}, u32[]{:S(2)}, u32[]{:S(2)}) collective-permute-start(f32[8,64,128]{2,1,0:T(8,128)S(1)} %multiply_add_fusion.2), channel_id=1, source_target_pairs={{0,8},{8,16},{16,24},{24,32},{32,40},{40,48},{48,56},{56,64},{64,7... | collective-permute-start | bytes 786440 | tf_op jit(solution)/shard_map/while/body/eval_jaxpr/ppermute | solution.py:17
  258.0 7.7 %collective-permute-start = (f32[8,64,128]{2,1,0:T(8,128)S(1)}, f32[8,64,128]{2,1,0:T(8,128)S(1)}, u32[]{:S(2)}, u32[]{:S(2)}) collective-permute-start(f32[8,64,128]{2,1,0:T(8,128)S(1)} %multiply_add_fusion.2), channel_id=1, source_target_pairs={{0,8},{8,16},{16,24},{24,32},{32,40},{40,48},{48,56},{56,64},{64,7... | collective-permute-start | bytes 786440 | tf_op jit(solution)/shard_map/while/body/eval_jaxpr/ppermute | solution.py:17
  265.8 7.7 %collective-permute-start = (f32[8,64,128]{2,1,0:T(8,128)S(1)}, f32[8,64,128]{2,1,0:T(8,128)S(1)}, u32[]{:S(2)}, u32[]{:S(2)}) collective-permute-start(f32[8,64,128]{2,1,0:T(8,128)S(1)} %multiply_add_fusion.2), channel_id=1, source_target_pairs={{0,8},{8,16},{16,24},{24,32},{32,40},{40,48},{48,56},{56,64},{64,7... | collective-permute-start | bytes 786440 | tf_op jit(solution)/shard_map/while/body/eval_jaxpr/ppermute | solution.py:17
  273.5 9.8 %collective-permute-start = (f32[8,64,128]{2,1,0:T(8,128)S(1)}, f32[8,64,128]{2,1,0:T(8,128)S(1)}, u32[]{:S(2)}, u32[]{:S(2)}) collective-permute-start(f32[8,64,128]{2,1,0:T(8,128)S(1)} %multiply_add_fusion.2), channel_id=1, source_target_pairs={{0,8},{8,16},{16,24},{24,32},{32,40},{40,48},{48,56},{56,64},{64,7... | collective-permute-start | bytes 786440 | tf_op jit(solution)/shard_map/while/body/eval_jaxpr/ppermute | solution.py:17
  283.4 9.8 %collective-permute-start = (f32[8,64,128]{2,1,0:T(8,128)S(1)}, f32[8,64,128]{2,1,0:T(8,128)S(1)}, u32[]{:S(2)}, u32[]{:S(2)}) collective-permute-start(f32[8,64,128]{2,1,0:T(8,128)S(1)} %multiply_add_fusion.2), channel_id=1, source_target_pairs={{0,8},{8,16},{16,24},{24,32},{32,40},{40,48},{48,56},{56,64},{64,7... | collective-permute-start | bytes 786440 | tf_op jit(solution)/shard_map/while/body/eval_jaxpr/ppermute | solution.py:17
  293.3 9.8 %collective-permute-start = (f32[8,64,128]{2,1,0:T(8,128)S(1)}, f32[8,64,128]{2,1,0:T(8,128)S(1)}, u32[]{:S(2)}, u32[]{:S(2)}) collective-permute-start(f32[8,64,128]{2,1,0:T(8,128)S(1)} %multiply_add_fusion.2), channel_id=1, source_target_pairs={{0,8},{8,16},{16,24},{24,32},{32,40},{40,48},{48,56},{56,64},{64,7... | collective-permute-start | bytes 786440 | tf_op jit(solution)/shard_map/while/body/eval_jaxpr/ppermute | solution.py:17
  303.2 9.8 %collective-permute-start = (f32[8,64,128]{2,1,0:T(8,128)S(1)}, f32[8,64,128]{2,1,0:T(8,128)S(1)}, u32[]{:S(2)}, u32[]{:S(2)}) collective-permute-start(f32[8,64,128]{2,1,0:T(8,128)S(1)} %multiply_add_fusion.2), channel_id=1, source_target_pairs={{0,8},{8,16},{16,24},{24,32},{32,40},{40,48},{48,56},{56,64},{64,7... | collective-permute-start | bytes 786440 | tf_op jit(solution)/shard_map/while/body/eval_jaxpr/ppermute | solution.py:17
  313.1 9.8 %collective-permute-start = (f32[8,64,128]{2,1,0:T(8,128)S(1)}, f32[8,64,128]{2,1,0:T(8,128)S(1)}, u32[]{:S(2)}, u32[]{:S(2)}) collective-permute-start(f32[8,64,128]{2,1,0:T(8,128)S(1)} %multiply_add_fusion.2), channel_id=1, source_target_pairs={{0,8},{8,16},{16,24},{24,32},{32,40},{40,48},{48,56},{56,64},{64,7... | collective-permute-start | bytes 786440 | tf_op jit(solution)/shard_map/while/body/eval_jaxpr/ppermute | solution.py:17
  323.0 9.8 %collective-permute-start = (f32[8,64,128]{2,1,0:T(8,128)S(1)}, f32[8,64,128]{2,1,0:T(8,128)S(1)}, u32[]{:S(2)}, u32[]{:S(2)}) collective-permute-start(f32[8,64,128]{2,1,0:T(8,128)S(1)} %multiply_add_fusion.2), channel_id=1, source_target_pairs={{0,8},{8,16},{16,24},{24,32},{32,40},{40,48},{48,56},{56,64},{64,7... | collective-permute-start | bytes 786440 | tf_op jit(solution)/shard_map/while/body/eval_jaxpr/ppermute | solution.py:17
  332.9 9.8 %collective-permute-start = (f32[8,64,128]{2,1,0:T(8,128)S(1)}, f32[8,64,128]{2,1,0:T(8,128)S(1)}, u32[]{:S(2)}, u32[]{:S(2)}) collective-permute-start(f32[8,64,128]{2,1,0:T(8,128)S(1)} %multiply_add_fusion.2), channel_id=1, source_target_pairs={{0,8},{8,16},{16,24},{24,32},{32,40},{40,48},{48,56},{56,64},{64,7... | collective-permute-start | bytes 786440 | tf_op jit(solution)/shard_map/while/body/eval_jaxpr/ppermute | solution.py:17
  342.8 9.8 %collective-permute-start = (f32[8,64,128]{2,1,0:T(8,128)S(1)}, f32[8,64,128]{2,1,0:T(8,128)S(1)}, u32[]{:S(2)}, u32[]{:S(2)}) collective-permute-start(f32[8,64,128]{2,1,0:T(8,128)S(1)} %multiply_add_fusion.2), channel_id=1, source_target_pairs={{0,8},{8,16},{16,24},{24,32},{32,40},{40,48},{48,56},{56,64},{64,7... | collective-permute-start | bytes 786440 | tf_op jit(solution)/shard_map/while/body/eval_jaxpr/ppermute | solution.py:17
  352.7 9.8 %collective-permute-start = (f32[8,64,128]{2,1,0:T(8,128)S(1)}, f32[8,64,128]{2,1,0:T(8,128)S(1)}, u32[]{:S(2)}, u32[]{:S(2)}) collective-permute-start(f32[8,64,128]{2,1,0:T(8,128)S(1)} %multiply_add_fusion.2), channel_id=1, source_target_pairs={{0,8},{8,16},{16,24},{24,32},{32,40},{40,48},{48,56},{56,64},{64,7... | collective-permute-start | bytes 786440 | tf_op jit(solution)/shard_map/while/body/eval_jaxpr/ppermute | solution.py:17
  362.6 9.8 %collective-permute-start = (f32[8,64,128]{2,1,0:T(8,128)S(1)}, f32[8,64,128]{2,1,0:T(8,128)S(1)}, u32[]{:S(2)}, u32[]{:S(2)}) collective-permute-start(f32[8,64,128]{2,1,0:T(8,128)S(1)} %multiply_add_fusion.2), channel_id=1, source_target_pairs={{0,8},{8,16},{16,24},{24,32},{32,40},{40,48},{48,56},{56,64},{64,7... | collective-permute-start | bytes 786440 | tf_op jit(solution)/shard_map/while/body/eval_jaxpr/ppermute | solution.py:17
  372.5 9.8 %collective-permute-start = (f32[8,64,128]{2,1,0:T(8,128)S(1)}, f32[8,64,128]{2,1,0:T(8,128)S(1)}, u32[]{:S(2)}, u32[]{:S(2)}) collective-permute-start(f32[8,64,128]{2,1,0:T(8,128)S(1)} %multiply_add_fusion.2), channel_id=1, source_target_pairs={{0,8},{8,16},{16,24},{24,32},{32,40},{40,48},{48,56},{56,64},{64,7... | collective-permute-start | bytes 786440 | tf_op jit(solution)/shard_map/while/body/eval_jaxpr/ppermute | solution.py:17
  382.4 9.8 %collective-permute-start = (f32[8,64,128]{2,1,0:T(8,128)S(1)}, f32[8,64,128]{2,1,0:T(8,128)S(1)}, u32[]{:S(2)}, u32[]{:S(2)}) collective-permute-start(f32[8,64,128]{2,1,0:T(8,128)S(1)} %multiply_add_fusion.2), channel_id=1, source_target_pairs={{0,8},{8,16},{16,24},{24,32},{32,40},{40,48},{48,56},{56,64},{64,7... | collective-permute-start | bytes 786440 | tf_op jit(solution)/shard_map/while/body/eval_jaxpr/ppermute | solution.py:17
  392.3 9.8 %collective-permute-start = (f32[8,64,128]{2,1,0:T(8,128)S(1)}, f32[8,64,128]{2,1,0:T(8,128)S(1)}, u32[]{:S(2)}, u32[]{:S(2)}) collective-permute-start(f32[8,64,128]{2,1,0:T(8,128)S(1)} %multiply_add_fusion.2), channel_id=1, source_target_pairs={{0,8},{8,16},{16,24},{24,32},{32,40},{40,48},{48,56},{56,64},{64,7... | collective-permute-start | bytes 786440 | tf_op jit(solution)/shard_map/while/body/eval_jaxpr/ppermute | solution.py:17
  402.2 9.8 %collective-permute-start = (f32[8,64,128]{2,1,0:T(8,128)S(1)}, f32[8,64,128]{2,1,0:T(8,128)S(1)}, u32[]{:S(2)}, u32[]{:S(2)}) collective-permute-start(f32[8,64,128]{2,1,0:T(8,128)S(1)} %multiply_add_fusion.2), channel_id=1, source_target_pairs={{0,8},{8,16},{16,24},{24,32},{32,40},{40,48},{48,56},{56,64},{64,7... | collective-permute-start | bytes 786440 | tf_op jit(solution)/shard_map/while/body/eval_jaxpr/ppermute | solution.py:17
  412.1 9.8 %collective-permute-start = (f32[8,64,128]{2,1,0:T(8,128)S(1)}, f32[8,64,128]{2,1,0:T(8,128)S(1)}, u32[]{:S(2)}, u32[]{:S(2)}) collective-permute-start(f32[8,64,128]{2,1,0:T(8,128)S(1)} %multiply_add_fusion.2), channel_id=1, source_target_pairs={{0,8},{8,16},{16,24},{24,32},{32,40},{40,48},{48,56},{56,64},{64,7... | collective-permute-start | bytes 786440 | tf_op jit(solution)/shard_map/while/body/eval_jaxpr/ppermute | solution.py:17
  422.0 9.8 %collective-permute-start = (f32[8,64,128]{2,1,0:T(8,128)S(1)}, f32[8,64,128]{2,1,0:T(8,128)S(1)}, u32[]{:S(2)}, u32[]{:S(2)}) collective-permute-start(f32[8,64,128]{2,1,0:T(8,128)S(1)} %multiply_add_fusion.2), channel_id=1, source_target_pairs={{0,8},{8,16},{16,24},{24,32},{32,40},{40,48},{48,56},{56,64},{64,7... | collective-permute-start | bytes 786440 | tf_op jit(solution)/shard_map/while/body/eval_jaxpr/ppermute | solution.py:17
  431.9 9.8 %collective-permute-start = (f32[8,64,128]{2,1,0:T(8,128)S(1)}, f32[8,64,128]{2,1,0:T(8,128)S(1)}, u32[]{:S(2)}, u32[]{:S(2)}) collective-permute-start(f32[8,64,128]{2,1,0:T(8,128)S(1)} %multiply_add_fusion.2), channel_id=1, source_target_pairs={{0,8},{8,16},{16,24},{24,32},{32,40},{40,48},{48,56},{56,64},{64,7... | collective-permute-start | bytes 786440 | tf_op jit(solution)/shard_map/while/body/eval_jaxpr/ppermute | solution.py:17
  441.8 9.8 %collective-permute-start = (f32[8,64,128]{2,1,0:T(8,128)S(1)}, f32[8,64,128]{2,1,0:T(8,128)S(1)}, u32[]{:S(2)}, u32[]{:S(2)}) collective-permute-start(f32[8,64,128]{2,1,0:T(8,128)S(1)} %multiply_add_fusion.2), channel_id=1, source_target_pairs={{0,8},{8,16},{16,24},{24,32},{32,40},{40,48},{48,56},{56,64},{64,7... | collective-permute-start | bytes 786440 | tf_op jit(solution)/shard_map/while/body/eval_jaxpr/ppermute | solution.py:17
  451.6 2.0 copy-start.2
  453.6 3.1 copy-start.7
Sparse Core Ops, SparseCore 0:
  9.1 57.7 all-gather.1
  461.2 81.0 reduce-scatter.1
where the time goes:
time: 553 us; the launch traced here: 549 us
  waiting for transfers between devices  231 us (42%)
  starting transfers between devices  190 us (34%)
  local copies, waits for them, and re-layouts  65.3 us (12%)
  matrix products  30.3 us (5%)
  other arithmetic  17.6 us (3%)
  between operations  13.6 us (2%)
    ppermute x32, starting transfers between devices, shifted(): lax.ppermute(value, axis, [(source, source + steps) for source in range(f...  190 us
    ppermute x32, waiting for transfers between devices, shifted(): lax.ppermute(value, axis, [(source, source + steps) for source in range(f...  92.5 us
    reduce_scatter x1, waiting for transfers between devices, per_device(): lax.psum_scatter(jnp.dot(hidden, w_out, preferred_element_type=jnp.float3...  81.2 us
    all_gather x1, waiting for transfers between devices, per_device(): lax.all_gather(tokens, 'tp', axis=0, tiled=True)  56.6 us
    dynamic_update_slice x8, local copies, waits for them, and re-layouts, run_spans(): lax.scan(span_pass, start_state, (split(head_values), split(b_rows), spli...  51.3 us
  transfers between devices with their start and end apart: 34, of which 34 were waited for; matrix products, arithmetic and copies ran while one was open for 1% of the time, Pallas kernels for 0%

commit v1 on v0

v1 whole, which is shorter than its diff:
```python
import functools
import math

import jax
import jax.numpy as jnp
from jax import lax
from jax.experimental import pallas as pl
from jax.experimental.pallas import tpu as pltpu
from jax.sharding import PartitionSpec as P

P_SIZE = 64
N = 128
CHUNK = 128
LOG2E = math.log2(math.e)
VMEM_LIMIT = 48 * 1024 * 1024

SLOT_OF_DISTANCE = (6, 0, 2, 4, 7, 5, 3, 1)
FIRST_SENT = (4, 3, -3)
LATER_SENT = (2, -2, 1, -1, 0)


def turned(value, axis, steps):
    count = lax.axis_size(axis)
    return lax.ppermute(value, axis, [(i, (i + steps) % count) for i in range(count)])


def next_block(value):
    count = lax.axis_size("ctx")
    return lax.ppermute(value, "ctx", [(i, i + 1) for i in range(count - 1)])


def rows_of_heads(per_head, heads):
    width = per_head.shape[1]
    return jnp.concatenate(
        [jnp.broadcast_to(per_head[h : h + 1], (P_SIZE, width)) for h in range(heads)], axis=0
    )


def project_kernel(count, *refs):
    pieces = refs[:count]
    w_ref = refs[count]
    out_ref, rows_ref = refs[-2:]

    @pl.when(pl.program_id(0) == 0)
    def _():
        at = 0
        for piece in pieces:
            size = piece.shape[0]
            rows_ref[at : at + size, :] = piece[...]
            at += size

    out_ref[...] = lax.dot_general(
        w_ref[...], rows_ref[...], (((1,), (1,)), ((), ())), preferred_element_type=jnp.float32
    ).astype(jnp.bfloat16)


def project(pieces, w_t, whole, row_count, block_at):
    cols, depth = w_t.shape
    rows = sum(piece.shape[0] for piece in pieces)
    tile = 432
    grid = (pl.cdiv(cols, tile),)
    in_specs = [pl.BlockSpec(piece.shape, lambda i: (0, 0)) for piece in pieces]
    in_specs.append(pl.BlockSpec((tile, depth), lambda i: (i, 0)))
    operands = list(pieces) + [w_t]
    aliases = {}
    if whole is not None:
        in_specs.append(pl.BlockSpec(memory_space=pl.ANY))
        operands.append(whole)
        aliases = {len(operands) - 1: 0}
    return pl.pallas_call(
        functools.partial(project_kernel, len(pieces)),
        grid=grid,
        in_specs=in_specs,
        out_specs=pl.BlockSpec((tile, rows), lambda i: (i, block_at)),
        out_shape=jax.ShapeDtypeStruct((cols, row_count), jnp.bfloat16),
        scratch_shapes=[pltpu.VMEM((rows, depth), jnp.bfloat16)],
        input_output_aliases=aliases,
        compiler_params=pltpu.CompilerParams(vmem_limit_bytes=VMEM_LIMIT),
        cost_estimate=pl.CostEstimate(
            flops=2 * rows * cols * depth,
            bytes_accessed=2 * (cols * depth + rows * depth + rows * cols),
            transcendentals=0,
        ),
        name="project",
    )(*operands)


def states_kernel(
    heads,
    perm_ref,
    proj_ref,
    halo_ref,
    taps_ref,
    bias_ref,
    head_ref,
    xbc_ref,
    run_ref,
    col_ref,
    cum_ref,
    local_ref,
    payload_ref,
    tail_ref,
    state_ref,
    total_ref,
):
    width = heads * P_SIZE
    step = pl.program_id(0)

    @pl.when(step == 0)
    def _():
        tail_ref[...] = halo_ref[...].astype(jnp.float32)
        state_ref[...] = jnp.zeros_like(state_ref)
        total_ref[...] = jnp.zeros_like(total_ref)

    lanes = lax.broadcasted_iota(jnp.int32, (P_SIZE, CHUNK), 1)
    xbc_width = xbc_ref.shape[0]
    for at in range(0, xbc_width, P_SIZE):
        raw = proj_ref[width + at : width + at + P_SIZE, :].astype(jnp.float32)
        tail = tail_ref[at : at + P_SIZE, :]
        acc = bias_ref[at : at + P_SIZE, :] + raw * taps_ref[3, at : at + P_SIZE, :]
        for back in (1, 2, 3):
            moved = jnp.where(
                lanes < back, pltpu.roll(tail, back, 1), pltpu.roll(raw, back, 1)
            )
            acc = acc + moved * taps_ref[3 - back, at : at + P_SIZE, :]
        tail_ref[at : at + P_SIZE, :] = raw
        xbc_ref[at : at + P_SIZE, :] = (acc * (0.5 * jnp.tanh(0.5 * acc) + 0.5)).astype(
            jnp.bfloat16
        )

    dt_raw = proj_ref[width + xbc_width : width + xbc_width + heads, :].astype(jnp.float32)
    shifted = dt_raw + head_ref[0]
    dt = jnp.maximum(shifted, 0.0) + jnp.log1p(jnp.exp(-jnp.abs(shifted)))
    run = -head_ref[1] * dt
    lane8 = lax.broadcasted_iota(jnp.int32, (heads, CHUNK), 1)
    reach = 1
    while reach < CHUNK:
        run = run + jnp.where(lane8 >= reach, pltpu.roll(run, reach, 1), 0.0)
        reach *= 2
    total = jnp.broadcast_to(run[:, CHUNK - 1 :], (heads, CHUNK))
    run_ref[...] = run
    col_ref[...] = run * LOG2E - jnp.log2(dt)
    cum_ref[...] = total_ref[...]
    factor = jnp.exp(total - run) * dt
    keep = jnp.exp(total)
    b_t = xbc_ref[width : width + N, :]
    inflow = (xbc_ref[:width, :].astype(jnp.float32) * rows_of_heads(factor, heads)).astype(
        jnp.bfloat16
    )
    added = lax.dot_general(
        inflow, b_t, (((1,), (1,)), ((), ())), preferred_element_type=jnp.float32
    )
    before = state_ref[...]
    local_ref[0] = before
    after = before * rows_of_heads(keep, heads) + added
    state_ref[...] = after
    all_total = total_ref[...] + total
    total_ref[...] = all_total

    @pl.when(step == pl.num_programs(0) - 1)
    def _():
        row = lax.broadcasted_iota(jnp.int32, (16, N), 0)
        high = all_total.astype(jnp.bfloat16).astype(jnp.float32)
        mid = (all_total - high).astype(jnp.bfloat16).astype(jnp.float32)
        low = all_total - high - mid
        pieces = width // 16
        for piece in range(pieces):
            h = piece * 16 // P_SIZE
            payload_ref[piece, :16, :] = after[piece * 16 : piece * 16 + 16].astype(jnp.bfloat16)
            parts = jnp.where(
                row == 0,
                jnp.broadcast_to(high[h : h + 1], (16, N)),
                jnp.where(
                    row == 1,
                    jnp.broadcast_to(mid[h : h + 1], (16, N)),
                    jnp.broadcast_to(low[h : h + 1], (16, N)),
                ),
            )
            payload_ref[piece, 16:, :] = parts.astype(jnp.bfloat16)


def chunk_states(perm, projected, halo, taps, bias, head_values):
    heads = head_values.shape[1]
    width = heads * P_SIZE
    cols, rows = projected.shape
    xbc_width = taps.shape[1]
    chunks = rows // CHUNK
    pieces = width // 16
    column = lambda j, perm: (0, j)
    return pl.pallas_call(
        functools.partial(states_kernel, heads),
        grid_spec=pltpu.PrefetchScalarGridSpec(
            num_scalar_prefetch=1,
            grid=(chunks,),
            in_specs=[
                pl.BlockSpec((cols, CHUNK), lambda j, perm: (0, perm[j])),
                pl.BlockSpec(halo.shape, lambda j, perm: (0, 0)),
                pl.BlockSpec(taps.shape, lambda j, perm: (0, 0, 0)),
                pl.BlockSpec(bias.shape, lambda j, perm: (0, 0)),
                pl.BlockSpec(head_values.shape, lambda j, perm: (0, 0, 0)),
            ],
            out_specs=[
                pl.BlockSpec((xbc_width, CHUNK), column),
                pl.BlockSpec((heads, CHUNK), column),
                pl.BlockSpec((heads, CHUNK), column),
                pl.BlockSpec((heads, CHUNK), column),
                pl.BlockSpec((1, width, N), lambda j, perm: (j, 0, 0)),
                pl.BlockSpec((pieces, 32, N), lambda j, perm: (0, 0, 0)),
            ],
            scratch_shapes=[
                pltpu.VMEM((xbc_width, CHUNK), jnp.float32),
                pltpu.VMEM((width, N), jnp.float32),
                pltpu.VMEM((heads, CHUNK), jnp.float32),
            ],
        ),
        out_shape=[
            jax.ShapeDtypeStruct((xbc_width, rows), jnp.bfloat16),
            jax.ShapeDtypeStruct((heads, rows), jnp.float32),
            jax.ShapeDtypeStruct((heads, rows), jnp.float32),
            jax.ShapeDtypeStruct((heads, rows), jnp.float32),
            jax.ShapeDtypeStruct((chunks, width, N), jnp.float32),
            jax.ShapeDtypeStruct((pieces, 32, N), jnp.bfloat16),
        ],
        compiler_params=pltpu.CompilerParams(vmem_limit_bytes=VMEM_LIMIT),
        cost_estimate=pl.CostEstimate(
            flops=2 * rows * width * N + 30 * rows * xbc_width,
            bytes_accessed=8 * 1024 * 1024,
            transcendentals=2 * rows * xbc_width,
        ),
        name="chunk_states",
    )(perm, projected, halo, taps, bias, head_values)


def inner_kernel(heads, perm_ref, gate_ref, xbc_ref, run_ref, col_ref, skip_ref, own_ref, open_ref):
    width = heads * P_SIZE
    b_t = xbc_ref[width : width + N, :]
    c_t = xbc_ref[width + N : width + 2 * N, :]
    scores = lax.dot_general(
        b_t, c_t, (((0,), (0,)), ((), ())), preferred_element_type=jnp.float32
    )
    sender = lax.broadcasted_iota(jnp.int32, (CHUNK, CHUNK), 0)
    taker = lax.broadcasted_iota(jnp.int32, (CHUNK, CHUNK), 1)
    lower = sender <= taker
    run = run_ref[...] * LOG2E
    columns = jnp.transpose(col_ref[...])
    for h in range(heads):
        top = h * P_SIZE
        spread = run[h : h + 1, :] - columns[:, h : h + 1]
        weights = jnp.where(lower, scores * jnp.exp2(spread), 0.0).astype(jnp.bfloat16)
        x_t = xbc_ref[top : top + P_SIZE, :]
        own = jnp.dot(x_t, weights, preferred_element_type=jnp.float32)
        own_ref[top : top + P_SIZE, :] = (
            own + skip_ref[top : top + P_SIZE, :] * x_t.astype(jnp.float32)
        )
        gate = gate_ref[top : top + P_SIZE, :].astype(jnp.float32)
        open_ref[top : top + P_SIZE, :] = gate * (0.5 * jnp.tanh(0.5 * gate) + 0.5)


def inner(perm, projected, xbc, run, col, skip):
    width = skip.shape[0]
    heads = width // P_SIZE
    rows = xbc.shape[1]
    chunks = rows // CHUNK
    column = lambda j, perm: (0, j)
    return pl.pallas_call(
        functools.partial(inner_kernel, heads),
        grid_spec=pltpu.PrefetchScalarGridSpec(
            num_scalar_prefetch=1,
            grid=(chunks,),
            in_specs=[
                pl.BlockSpec((width, CHUNK), lambda j, perm: (0, perm[j])),
                pl.BlockSpec((xbc.shape[0], CHUNK), column),
                pl.BlockSpec((heads, CHUNK), column),
                pl.BlockSpec((heads, CHUNK), column),
                pl.BlockSpec((width, CHUNK), lambda j, perm: (0, 0)),
            ],
            out_specs=[
                pl.BlockSpec((width, CHUNK), column),
                pl.BlockSpec((width, CHUNK), column),
            ],
        ),
        out_shape=[
            jax.ShapeDtypeStruct((width, rows), jnp.float32),
            jax.ShapeDtypeStruct((width, rows), jnp.float32),
        ],
        compiler_params=pltpu.CompilerParams(vmem_limit_bytes=VMEM_LIMIT),
        cost_estimate=pl.CostEstimate(
            flops=2 * rows * CHUNK * (width + N) + 8 * rows * CHUNK * heads,
            bytes_accessed=8 * 1024 * 1024,
            transcendentals=rows * (CHUNK * heads + width),
        ),
        name="inner",
    )(perm, projected, xbc, run, col, skip)


def prefix_kernel(got_ref, out_ref):
    count = got_ref.shape[0]
    state = jnp.zeros((16, N), jnp.float32)
    for c in range(count):
        out_ref[c] = state.astype(jnp.bfloat16)
        if c < count - 1:
            tail = got_ref[c, 16:, :].astype(jnp.float32)
            log_decay = tail[0:1] + tail[1:2] + tail[2:3]
            state = state * jnp.exp(log_decay) + got_ref[c, :16, :].astype(jnp.float32)


def prefix(got):
    count = got.shape[0]
    return pl.pallas_call(
        prefix_kernel,
        out_shape=jax.ShapeDtypeStruct((count, 16, N), jnp.bfloat16),
        name="prefix",
    )(got)


def finish_kernel(
    heads,
    order_ref,
    own_ref,
    open_ref,
    c_ref,
    run_ref,
    cum_ref,
    local_ref,
    state_ref,
    gain_ref,
    w_ref,
    out_ref,
    u_ref,
):
    width = heads * P_SIZE
    keep = jnp.exp(cum_ref[...])
    start = (
        local_ref[0] + state_ref[...].astype(jnp.float32) * rows_of_heads(keep, heads)
    ).astype(jnp.bfloat16)
    carried = jnp.dot(start, c_ref[...], preferred_element_type=jnp.float32)
    grown = jnp.exp(run_ref[...])
    squares = jnp.zeros((1, CHUNK), jnp.float32)
    for h in range(heads):
        part = slice(h * P_SIZE, (h + 1) * P_SIZE)
        u = (own_ref[part, :] + carried[part, :] * grown[h : h + 1, :]) * open_ref[part, :]
        squares = squares + jnp.sum(u * u, axis=0, keepdims=True)
        u_ref[part, :] = u
    scale = lax.rsqrt(squares * (1.0 / width) + 1e-05)
    hidden = (u_ref[...] * scale * gain_ref[...]).astype(jnp.bfloat16)
    out_ref[0] = lax.dot_general(
        hidden, w_ref[...], (((0,), (0,)), ((), ())), preferred_element_type=jnp.float32
    ).astype(jnp.bfloat16)


def finish(order, own, opened, xbc, run, cum, local, state, gain, w_out):
    width, rows = own.shape
    heads = width // P_SIZE
    count = order.shape[0]
    out_width = w_out.shape[1]
    column = lambda j, order: (0, order[j])
    fixed = lambda j, order: (0, 0)
    c_block = (width + N) // N
    return pl.pallas_call(
        functools.partial(finish_kernel, heads),
        grid_spec=pltpu.PrefetchScalarGridSpec(
            num_scalar_prefetch=1,
            grid=(count,),
            in_specs=[
                pl.BlockSpec((width, CHUNK), column),
                pl.BlockSpec((width, CHUNK), column),
                pl.BlockSpec((N, CHUNK), lambda j, order: (c_block, order[j])),
                pl.BlockSpec((heads, CHUNK), column),
                pl.BlockSpec((heads, CHUNK), column),
                pl.BlockSpec((1, width, N), lambda j, order: (order[j], 0, 0)),
                pl.BlockSpec((width, N), fixed),
                pl.BlockSpec((width, CHUNK), fixed),
                pl.BlockSpec((width, out_width), fixed),
            ],
            out_specs=pl.BlockSpec((1, CHUNK, out_width), lambda j, order: (j, 0, 0)),
            scratch_shapes=[pltpu.VMEM((width, CHUNK), jnp.float32)],
        ),
        out_shape=jax.ShapeDtypeStruct((count, CHUNK, out_width), jnp.bfloat16),
        compiler_params=pltpu.CompilerParams(vmem_limit_bytes=VMEM_LIMIT),
        cost_estimate=pl.CostEstimate(
            flops=2 * count * CHUNK * width * (out_width + N),
            bytes_accessed=2 * width * out_width + count * 1024 * 1024,
            transcendentals=0,
        ),
        name="finish",
    )(order, own, opened, xbc, run, cum, local, state, gain, w_out)


def per_device(
    tokens, w_in, conv_weight, conv_bias, dt_bias, decay_rate, skip_scale, norm_gain, w_out
):
    me = lax.axis_index("tp")
    n_tp = lax.axis_size("tp")
    width = norm_gain.shape[0]
    heads = decay_rate.shape[0]
    rows = tokens.shape[0] * n_tp
    half = tokens.shape[0] // 2
    w_t = jnp.transpose(w_in.reshape(w_in.shape[0], w_in.shape[2]))
    xbc_width = conv_weight.shape[2]

    edge = lax.all_gather(next_block(tokens[-8:]), "tp", axis=0)[n_tp - 1]
    halo = lax.dot_general(
        w_t[width : width + xbc_width], edge, (((1,), (1,)), ((), ())),
        preferred_element_type=jnp.float32,
    ).astype(jnp.bfloat16)
    halo = jnp.pad(halo, ((0, 0), (CHUNK - 8, 0)))

    taps = jnp.broadcast_to(
        conv_weight.reshape(conv_weight.shape[0], xbc_width, 1).astype(jnp.float32),
        (conv_weight.shape[0], xbc_width, CHUNK),
    )
    bias = jnp.broadcast_to(
        conv_bias.reshape(xbc_width, 1).astype(jnp.float32), (xbc_width, CHUNK)
    )
    head_values = jnp.broadcast_to(
        jnp.stack([dt_bias, decay_rate])[:, :, None], (2, heads, CHUNK)
    )
    skip = jnp.broadcast_to(jnp.repeat(skip_scale, P_SIZE)[:, None], (width, CHUNK))
    gain = jnp.broadcast_to(norm_gain[:, None], (width, CHUNK))
    perm = jnp.asarray(SLOT_OF_DISTANCE, jnp.int32)[(jnp.arange(n_tp) - me) % n_tp]

    right = [tokens[:half], tokens[half:]]
    left = [tokens[:half], tokens[half:]]
    projected = project([tokens], w_t, None, rows, 6)
    for hop in range(1, 4):
        right = [turned(right[0], "tp", 1), turned(right[1], "tp", 1)]
        left = [turned(left[0], "tp", -1), turned(left[1], "tp", -1)]
        projected = project(left + right, w_t, projected, rows, hop - 1)
    last = [turned(right[0], "tp", 1), turned(left[1], "tp", -1)]
    projected = project(last, w_t, projected, rows, 7)

    xbc, run, col, cum, local, payload = chunk_states(
        perm, projected, halo, taps, bias, head_values
    )
    got = lax.all_to_all(payload, "ctx", 0, 0, tiled=True)
    own, opened = inner(perm, projected, xbc, run, col, skip)
    state = lax.all_to_all(prefix(got), "ctx", 0, 0, tiled=True).reshape(width, N)

    def finished(distances):
        order = ((me + jnp.asarray(distances, jnp.int32)) % n_tp).astype(jnp.int32)
        return finish(order, own, opened, xbc, run, cum, local, state, gain, w_out)

    first, later = finished(FIRST_SENT), finished(LATER_SENT)
    blocks = {d: first[i] for i, d in enumerate(FIRST_SENT)}
    blocks.update({d: later[i] for i, d in enumerate(LATER_SENT)})

    def block(distance, part):
        return blocks[distance][part * half : (part + 1) * half]

    def plus(moving, distance, part):
        return (
            moving.astype(jnp.float32) + block(distance, part).astype(jnp.float32)
        ).astype(jnp.bfloat16)

    r0, l1 = turned(block(4, 0), "tp", 1), turned(block(4, 1), "tp", -1)
    r1, l0 = turned(block(3, 1), "tp", 1), turned(block(-3, 0), "tp", -1)
    for k in (3, 2, 1):
        r0 = turned(plus(r0, k, 0), "tp", 1)
        l1 = turned(plus(l1, -k, 1), "tp", -1)
        if k > 1:
            r1 = turned(plus(r1, k - 1, 1), "tp", 1)
            l0 = turned(plus(l0, 1 - k, 0), "tp", -1)
    top = r0.astype(jnp.float32) + l0.astype(jnp.float32) + block(0, 0).astype(jnp.float32)
    bottom = r1.astype(jnp.float32) + l1.astype(jnp.float32) + block(0, 1).astype(jnp.float32)
    return jnp.concatenate([top, bottom], axis=0).astype(jnp.bfloat16)


def solution(mesh):
    placed = (
        P(("ctx", "tp"), None),
        P(None, "tp", None),
        P(None, "tp", None),
        P("tp", None),
        P("tp"),
        P("tp"),
        P("tp"),
        P("tp"),
        P("tp", None),
    )
    return jax.shard_map(
        per_device, mesh=mesh, in_specs=placed, out_specs=P(("ctx", "tp"), None), check_vma=False
    )
```

time: 553 us -> 194 us (0.35)
  waiting for transfers between devices: 231 us -> 24.1 us
  starting transfers between devices: 190 us -> 52.3 us
  Pallas kernels: 0 us -> 54.8 us
  local copies, waits for them, and re-layouts: 65.3 us -> 14.4 us
  blocking collectives: 0 us -> 40.2 us
  matrix products: 30.3 us -> 0.91 us
  between operations: 13.6 us -> 0.37 us
  other arithmetic: 17.6 us -> 5.44 us
    ppermute x32 -> x29, starting transfers between devices: 190 us -> 47.2 us  [the longest x28 45.3 us: turned(): lax.ppermute(value, axis, [(i, (i + steps) % count) for i in range(count)])]
    reduce_scatter x1 -> x0, waiting for transfers between devices: 81.2 us -> none  [per_device(): lax.psum_scatter(jnp.dot(hidden, w_out, preferred_element_type=jnp.float3...]
    ppermute x32 -> x29, waiting for transfers between devices: 92.5 us -> 24.1 us  [the longest x28 24.1 us: turned(): lax.ppermute(value, axis, [(i, (i + steps) % count) for i in range(count)])]
    all_gather x1 -> x0, waiting for transfers between devices: 56.6 us -> none  [per_device(): lax.all_gather(tokens, 'tp', axis=0, tiled=True)]
    pallas_call x0 -> x10, Pallas kernels: none -> 54.8 us  [the longest x5 24.3 us: project(): pl.pallas_call(functools.partial(project_kernel, len(pieces)), grid=grid,...]
    dynamic_update_slice x8 -> x0, local copies, waits for them, and re-layouts: 51.3 us -> none  [run_spans(): lax.scan(span_pass, start_state, (split(head_values), split(b_rows), spli...]
    dot_general x19 -> x1, matrix products: 30.3 us -> 0.91 us  [per_device(): lax.dot_general(w_t[width:width + xbc_width], edge, (((1,), (1,)), ((), (...]
    all_gather x0 -> x1, blocking collectives: none -> 25 us  [per_device(): edge = lax.all_gather(next_block(tokens[-8:]), 'tp', axis=0)[n_tp - 1]]
  transfers between devices with their start and end apart: 34 -> 30, of which waited for: 34 -> 8; matrix products, arithmetic and copies ran while one was open for 1% -> 4% of each run, Pallas kernels for 0% -> 18%
where the time goes in v1:
time: 194 us; the launch traced here: 192 us
  Pallas kernels  54.8 us (28%)
  starting transfers between devices  52.3 us (27%)
  blocking collectives  40.2 us (21%)
  waiting for transfers between devices  24.1 us (12%)
  local copies, waits for them, and re-layouts  14.4 us (7%)
  other arithmetic  5.44 us (3%)
    ppermute x28, starting transfers between devices, turned(): lax.ppermute(value, axis, [(i, (i + steps) % count) for i in range(count)])  45.3 us
    all_gather x1, blocking collectives, per_device(): edge = lax.all_gather(next_block(tokens[-8:]), 'tp', axis=0)[n_tp - 1]  25 us
    pallas_call x5, Pallas kernels, project(): pl.pallas_call(functools.partial(project_kernel, len(pieces)), grid=grid,...  24.3 us
    ppermute x28, waiting for transfers between devices, turned(): lax.ppermute(value, axis, [(i, (i + steps) % count) for i in range(count)])  24.1 us
    all_to_all x1, blocking collectives, per_device(): got = lax.all_to_all(payload, 'ctx', 0, 0, tiled=True)  15.2 us
    pallas_call x2, Pallas kernels, finish(): pl.pallas_call(functools.partial(finish_kernel, heads), grid_spec=pltpu.P...  12.7 us
    pallas_call x1, Pallas kernels, chunk_states(): pl.pallas_call(functools.partial(states_kernel, heads), grid_spec=pltpu.P...  9.24 us
    unnamed x24, local copies, waits for them, and re-layouts  8.19 us
  transfers between devices with their start and end apart: 30, of which 8 were waited for; matrix products, arithmetic and copies ran while one was open for 4% of the time, Pallas kernels for 18%

profile of v1, /device:TPU:2, one launch (start us, length us, event | category | flops | bytes accessed | tf_op | source)
XLA Modules:
  0.0 192.4 jit_solution(4679970544477460130)
XLA Ops:
  0.0 1.1 fusion.22
  1.1 2.0 %collective-permute-start = (bf16[64,2048]{1,0:T(8,128)(2,1)S(1)}, bf16[64,2048]{1,0:T(8,128)(2,1)S(1)}, u32[]{:S(2)}, u32[]{:S(2)}) collective-permute-start(bf16[64,2048]{1,0:T(8,128)(2,1)S(1)} %get-tuple-element.38), channel_id=1, source_target_pairs={{0,1},{1,2},{2,3},{3,4},{4,5},{5,6},{6,7},{7,0},{8,9},{9,10},{10,1... | collective-permute-start | bytes 786440 | tf_op jit(solution)/shard_map/ppermute | solution.py:24
  3.1 4.0 %collective-permute-start.8 = (bf16[64,2048]{1,0:T(8,128)(2,1)S(1)}, bf16[64,2048]{1,0:T(8,128)(2,1)S(1)}, u32[]{:S(2)}, u32[]{:S(2)}) collective-permute-start(bf16[64,2048]{1,0:T(8,128)(2,1)S(1)} %get-tuple-element.38), channel_id=1, source_target_pairs={{0,7},{1,0},{2,1},{3,2},{4,3},{5,4},{6,5},{7,6},{8,15},{9,8},{10,9... | collective-permute-start | bytes 786440 | tf_op jit(solution)/shard_map/ppermute | solution.py:24
  7.1 1.9 %collective-permute-start.4 = (bf16[64,2048]{1,0:T(8,128)(2,1)S(1)}, bf16[64,2048]{1,0:T(8,128)(2,1)S(1)}, u32[]{:S(2)}, u32[]{:S(2)}) collective-permute-start(bf16[64,2048]{1,0:T(8,128)(2,1)S(1)} %get-tuple-element.37), channel_id=1, source_target_pairs={{0,7},{1,0},{2,1},{3,2},{4,3},{5,4},{6,5},{7,6},{8,15},{9,8},{10,9... | collective-permute-start | bytes 786440 | tf_op jit(solution)/shard_map/ppermute | solution.py:24
  9.1 0.8 slice.116
  9.9 1.9 collective-permute-start.14
  11.8 0.7 convert_reduce_fusion
  12.5 1.3 gather_fusion
  13.8 0.7 bitcast_convert_fusion
  14.5 3.7 %collective-permute-done.4.refs_1_ = bf16[64,2048]{1,0:T(8,128)(2,1)S(1)} collective-permute-done((bf16[64,2048]{1,0:T(8,128)(2,1)S(1)}, bf16[64,2048]{1,0:T(8,128)(2,1)S(1)}, u32[]{:S(2)}, u32[]{:S(2)}) %collective-permute-start.4) | collective-permute-done | bytes 262176 | tf_op jit(solution)/shard_map/ppermute | solution.py:24
  18.3 3.7 %collective-permute-start.5 = (bf16[64,2048]{1,0:T(8,128)(2,1)S(1)}, bf16[64,2048]{1,0:T(8,128)(2,1)}, u32[]{:S(2)}, u32[]{:S(2)}) collective-permute-start(bf16[64,2048]{1,0:T(8,128)(2,1)S(1)} %collective-permute-done.4.refs_1_), channel_id=1, source_target_pairs={{0,7},{1,0},{2,1},{3,2},{4,3},{5,4},{6,5},{7,6},{8,15},{9,8},{10,9... | collective-permute-start | bytes 786440 | tf_op jit(solution)/shard_map/ppermute | solution.py:24
  22.0 0.4 collective-permute-start.9
  22.4 1.6 collective-permute-start.12
  24.0 0.7 pad_maximum_fusion.1
  24.7 1.0 copy-done.5
  25.7 5.0 %project.5.refs_5_ = bf16[1288,1024]{1,0:T(8,128)(2,1)S(1)} custom-call(bf16[128,2048]{1,0:T(8,128)(2,1)S(1)} %copy-done.5, bf16[1288,2048]{1,0:T(8,128)(2,1)} %bitcast.81), custom_call_target="tpu_custom_call" | custom-call | flops 675282944 | bytes 6129664 | tf_op jit(solution)/shard_map/project/pallas_call | solution.py:70
  30.8 25.0 %all-gather = bf16[64,2048]{1,0:T(8,128)(2,1)S(1)} all-gather(bf16[8,2048]{1,0:T(8,128)(2,1)S(1)} %collective-permute-done.14), channel_id=2, replica_groups=mesh['ctx'=32,'tp'=8] {'tp'}, dimensions={0}, use_global_device_ids=true | all-gather | bytes 294912 | tf_op jit(solution)/shard_map/all_gather | solution.py:401
  55.8 0.8 collective-permute-start.2
  56.6 2.5 %collective-permute-start.6 = (bf16[64,2048]{1,0:T(8,128)(2,1)}, bf16[64,2048]{1,0:T(8,128)(2,1)}, u32[]{:S(2)}, u32[]{:S(2)}) collective-permute-start(bf16[64,2048]{1,0:T(8,128)(2,1)} %collective-permute-done.5.refs_1_), channel_id=1, source_target_pairs={{0,7},{1,0},{2,1},{3,2},{4,3},{5,4},{6,5},{7,6},{8,15},{9,8},{10,9... | collective-permute-start | bytes 786440 | tf_op jit(solution)/shard_map/ppermute | solution.py:24
  59.0 0.4 collective-permute-start.10
  59.5 1.6 collective-permute-start.13
  61.1 0.9 fusion.2
  62.0 0.8 copy.19
  62.8 1.0 pad.4.halo_ref
  63.9 0.6 collective-permute-done.2.refs_2_
  64.5 3.2 %collective-permute-start.7 = (bf16[64,2048]{1,0:T(8,128)(2,1)}, bf16[64,2048]{1,0:T(8,128)(2,1)S(1)}, u32[]{:S(2)}, u32[]{:S(2)}) collective-permute-start(bf16[64,2048]{1,0:T(8,128)(2,1)} %collective-permute-done.6.refs_1_), channel_id=1, source_target_pairs={{0,7},{1,0},{2,1},{3,2},{4,3},{5,4},{6,5},{7,6},{8,15},{9,8},{10,9... | collective-permute-start | bytes 786440 | tf_op jit(solution)/shard_map/ppermute | solution.py:24
  67.8 4.7 %project.6.refs_5_ = bf16[1288,1024]{1,0:T(8,128)(2,1)S(1)} custom-call(bf16[64,2048]{1,0:T(8,128)(2,1)S(1)} %collective-permute-done.8.refs_0_, bf16[64,2048]{1,0:T(8,128)(2,1)S(1)} %collective-permute-done.4.refs_1_, bf16[64,2048]{1,0:T(8,128)(2,1)S(1)} %collective-permute-done.refs_2_, ...), custom_call_target="tpu_custom_call", output_to_operand_aliasing={{}: (5, {})} | custom-call | flops 1350565888 | bytes 6983680 | tf_op jit(solution)/shard_map/project/pallas_call | solution.py:70
  72.5 5.0 %project.7.refs_5_ = bf16[1288,1024]{1,0:T(8,128)(2,1)S(1)} custom-call(bf16[64,2048]{1,0:T(8,128)(2,1)} %collective-permute-done.9.refs_0_, bf16[64,2048]{1,0:T(8,128)(2,1)} %collective-permute-done.5.refs_1_, bf16[64,2048]{1,0:T(8,128)(2,1)} %collective-permute-done.1.refs_2_, ...), custom_call_target="tpu_custom_call", output_to_operand_aliasing={{}: (5, {})} | custom-call | flops 1350565888 | bytes 6983680 | tf_op jit(solution)/shard_map/project/pallas_call | solution.py:70
  77.5 5.0 %project.8.refs_3_ = bf16[1288,1024]{1,0:T(8,128)(2,1)S(1)} custom-call(bf16[64,2048]{1,0:T(8,128)(2,1)} %collective-permute-done.10.refs_0_, bf16[64,2048]{1,0:T(8,128)(2,1)} %collective-permute-done.6.refs_1_, bf16[64,2048]{1,0:T(8,128)(2,1)} %collective-permute-done.2.refs_2_, ...), custom_call_target="tpu_custom_call", output_to_operand_aliasing={{}: (5, {})} | custom-call | flops 1350565888 | bytes 6983680 | tf_op jit(solution)/shard_map/project/pallas_call | solution.py:70
  82.5 4.6 %project.9.proj_ref.gate_ref = bf16[1288,1024]{1,0:T(8,128)(2,1)S(1)} custom-call(bf16[64,2048]{1,0:T(8,128)(2,1)S(1)} %collective-permute-done.3.refs_0_, bf16[64,2048]{1,0:T(8,128)(2,1)S(1)} %collective-permute-done.7.refs_1_, bf16[1288,2048]{1,0:T(8,128)(2,1)} %bitcast.85, bf16[1288,1024]{1,0:T(8,128)(2,1)S(1)} %project.8.refs_3_), custom_call_target="tpu_custom_call", output_to_operand_aliasing={{}: (3, {})} | custom-call | flops 675282944 | bytes 6129664 | tf_op jit(solution)/shard_map/project/pallas_call | solution.py:70
  87.2 1.5 copy-done
  88.7 0.5 broadcast_in_dim.14.taps_ref
  89.1 0.2 broadcast_in_dim.15.bias_ref
  89.4 9.2 %chunk_states.1 = (bf16[768,1024]{1,0:T(8,128)(2,1)S(1)}, f32[8,1024]{1,0:T(8,128)S(1)}, f32[8,1024]{1,0:T(8,128)S(1)}, f32[8,1024]{1,0:T(8,128)S(1)}, f32[8,512...) custom-call(s32[8]{0:T(128)S(1)} %gather_fusion, bf16[1288,1024]{1,0:T(8,128)(2,1)} %copy-done, ...), custom_call_target="tpu_custom_call" | custom-call | flops 157810688 | bytes 8388608 | tf_op jit(solution)/shard_map/chunk_states/pallas_call | solution.py:190
  98.6 1.3 copy-done.1
  100.0 15.2 %all_to_all.10.got_ref = bf16[32,32,128]{2,1,0:T(8,128)(2,1)} all-to-all(bf16[32,32,128]{2,1,0:T(8,128)(2,1)S(1)} %get-tuple-element.20), channel_id=1, replica_groups=mesh['ctx'=32,'tp'=8] {'ctx'}, dimensions={0} | all-to-all | bytes 524288 | tf_op jit(solution)/shard_map/all_to_all | solution.py:435
  115.2 1.7 prefix.1
  116.8 5.1 %all-to-all-start.1 = ((bf16[32,16,128]{2,1,0:T(8,128)(2,1)}), bf16[32,16,128]{2,1,0:T(8,128)(2,1)S(1)}, u32[]{:S(2)}, u32[]{:S(2)}) async-start(bf16[32,16,128]{2,1,0:T(8,128)(2,1)} %prefix.1), calls=%async_computation.1 | async-start | bytes 262144 | tf_op jit(solution)/shard_map/all_to_all | solution.py:437
  122.1 0.1 broadcast_in_dim.38.skip_ref
  122.3 6.8 %inner.1 = (f32[512,1024]{1,0:T(8,128)S(1)}, f32[512,1024]{1,0:T(8,128)S(1)}) custom-call(s32[8]{0:T(128)S(1)} %gather_fusion, bf16[1288,1024]{1,0:T(8,128)(2,1)} %copy-done, bf16[768,1024]{1,0:T(8,128)(2,1)S(1)} %get-tuple-element.13.xbc_ref.c_ref, f32[8,1024]{1,0:T(8,128)S(1)} %get-tuple-element.14.run_ref, f32[8,1024]{1,0:T(8,128)S(1)} %get-tuple-element.15.col_ref, ...), custom_call_target="tpu_custom_call" | custom-call | flops 176160768 | bytes 8388608 | tf_op jit(solution)/shard_map/inner/pallas_call | solution.py:265
  129.1 1.4 copy-done.2
  130.5 1.3 copy-done.4
  132.0 1.6 copy-done.3
  133.6 4.9 %finish.2 = bf16[3,128,2048]{2,1,0:T(8,128)(2,1)S(1)} custom-call(s32[3]{0:T(128)S(1)} %and_select_fusion.2.order_ref, f32[512,1024]{1,0:T(8,128)S(1)} %copy-done.3, f32[512,1024]{1,0:T(8,128)} %copy-done.4, bf16[768,1024]{1,0:T(8,128)(2,1)S(1)} %get-tuple-element.13.xbc_ref.c_ref, f32[8,1024]{1,0:T(8,128)S(1)} %get-tuple-element.14.run_ref, ...), custom_call_target="tpu_custom_call" | custom-call | flops 855638016 | bytes 5242880 | tf_op jit(solution)/shard_map/finish/pallas_call | solution.py:359
  138.7 3.2 %collective-permute-start.25 = (bf16[64,2048]{1,0:T(8,128)(2,1)S(1)}, bf16[64,2048]{1,0:T(8,128)(2,1)S(1)}, u32[]{:S(2)}, u32[]{:S(2)}) collective-permute-start(bf16[64,2048]{1,0:T(8,128)(2,1)S(1)} %get-tuple-element.34), channel_id=1, source_target_pairs={{0,7},{1,0},{2,1},{3,2},{4,3},{5,4},{6,5},{7,6},{8,15},{9,8},{10,9... | collective-permute-start | bytes 786440 | tf_op jit(solution)/shard_map/ppermute | solution.py:24
  141.9 3.2 %collective-permute-start.19 = (bf16[64,2048]{1,0:T(8,128)(2,1)S(1)}, bf16[64,2048]{1,0:T(8,128)(2,1)S(1)}, u32[]{:S(2)}, u32[]{:S(2)}) collective-permute-start(bf16[64,2048]{1,0:T(8,128)(2,1)S(1)} %get-tuple-element.36), channel_id=1, source_target_pairs={{0,7},{1,0},{2,1},{3,2},{4,3},{5,4},{6,5},{7,6},{8,15},{9,8},{10,9... | collective-permute-start | bytes 786440 | tf_op jit(solution)/shard_map/ppermute | solution.py:24
  145.1 3.9 %collective-permute-done.15 = bf16[64,2048]{1,0:T(8,128)(2,1)S(1)} collective-permute-done((bf16[64,2048]{1,0:T(8,128)(2,1)S(1)}, bf16[64,2048]{1,0:T(8,128)(2,1)S(1)}, u32[]{:S(2)}, u32[]{:S(2)}) %collective-permute-start.15) | collective-permute-done | bytes 262176 | tf_op jit(solution)/shard_map/ppermute | solution.py:24
  149.0 0.1 fusion.16
  149.3 3.3 %collective-permute-start.26 = (bf16[64,2048]{1,0:T(8,128)(2,1)S(1)}, bf16[64,2048]{1,0:T(8,128)(2,1)S(1)}, u32[]{:S(2)}, u32[]{:S(2)}) collective-permute-start(bf16[64,2048]{1,0:T(8,128)(2,1)S(1)} %get-tuple-element.32), channel_id=1, source_target_pairs={{0,7},{1,0},{2,1},{3,2},{4,3},{5,4},{6,5},{7,6},{8,15},{9,8},{10,9... | collective-permute-start | bytes 786440 | tf_op jit(solution)/shard_map/ppermute | solution.py:24
  152.6 7.8 %finish.3 = bf16[5,128,2048]{2,1,0:T(8,128)(2,1)} custom-call(s32[5]{0:T(128)S(1)} %and_select_fusion.order_ref, f32[512,1024]{1,0:T(8,128)S(1)} %copy-done.3, f32[512,1024]{1,0:T(8,128)} %copy-done.4, bf16[768,1024]{1,0:T(8,128)(2,1)S(1)} %get-tuple-element.13.xbc_ref.c_ref, f32[8,1024]{1,0:T(8,128)S(1)} %get-tuple-element.14.run_ref, ...), custom_call_target="tpu_custom_call" | custom-call | flops 1426063360 | bytes 7340032 | tf_op jit(solution)/shard_map/finish/pallas_call | solution.py:359
  160.4 1.7 fusion.15
  162.1 0.3 collective-permute-start.17
  162.4 3.2 %collective-permute-start.27 = (bf16[64,2048]{1,0:T(8,128)(2,1)S(1)}, bf16[64,2048]{1,0:T(8,128)(2,1)S(1)}, u32[]{:S(2)}, u32[]{:S(2)}) collective-permute-start(bf16[64,2048]{1,0:T(8,128)(2,1)S(1)} %get-tuple-element.28), channel_id=1, source_target_pairs={{0,7},{1,0},{2,1},{3,2},{4,3},{5,4},{6,5},{7,6},{8,15},{9,8},{10,9... | collective-permute-start | bytes 786440 | tf_op jit(solution)/shard_map/ppermute | solution.py:24
  165.6 3.2 %collective-permute-start.20 = (bf16[64,2048]{1,0:T(8,128)(2,1)S(1)}, bf16[64,2048]{1,0:T(8,128)(2,1)S(1)}, u32[]{:S(2)}, u32[]{:S(2)}) collective-permute-start(bf16[64,2048]{1,0:T(8,128)(2,1)S(1)} %get-tuple-element.30), channel_id=1, source_target_pairs={{0,7},{1,0},{2,1},{3,2},{4,3},{5,4},{6,5},{7,6},{8,15},{9,8},{10,9... | collective-permute-start | bytes 786440 | tf_op jit(solution)/shard_map/ppermute | solution.py:24
  168.9 4.0 %collective-permute-done.17 = bf16[64,2048]{1,0:T(8,128)(2,1)S(1)} collective-permute-done((bf16[64,2048]{1,0:T(8,128)(2,1)S(1)}, bf16[64,2048]{1,0:T(8,128)(2,1)S(1)}, u32[]{:S(2)}, u32[]{:S(2)}) %collective-permute-start.17) | collective-permute-done | bytes 262176 | tf_op jit(solution)/shard_map/ppermute | solution.py:24
  172.9 3.0 %collective-permute-done.23 = bf16[64,2048]{1,0:T(8,128)(2,1)S(1)} collective-permute-done((bf16[64,2048]{1,0:T(8,128)(2,1)S(1)}, bf16[64,2048]{1,0:T(8,128)(2,1)S(1)}, u32[]{:S(2)}, u32[]{:S(2)}) %collective-permute-start.23) | collective-permute-done | bytes 262176 | tf_op jit(solution)/shard_map/ppermute | solution.py:24
  175.9 0.4 fusion.14
  176.3 3.0 %collective-permute-start.21 = (bf16[64,2048]{1,0:T(8,128)(2,1)S(1)}, bf16[64,2048]{1,0:T(8,128)(2,1)S(1)}, u32[]{:S(2)}, u32[]{:S(2)}) collective-permute-start(bf16[64,2048]{1,0:T(8,128)(2,1)S(1)} %get-tuple-element.26), channel_id=1, source_target_pairs={{0,7},{1,0},{2,1},{3,2},{4,3},{5,4},{6,5},{7,6},{8,15},{9,8},{10,9... | collective-permute-start | bytes 786440 | tf_op jit(solution)/shard_map/ppermute | solution.py:24
  179.3 3.2 %collective-permute-start.28 = (bf16[64,2048]{1,0:T(8,128)(2,1)S(1)}, bf16[64,2048]{1,0:T(8,128)(2,1)S(1)}, u32[]{:S(2)}, u32[]{:S(2)}) collective-permute-start(bf16[64,2048]{1,0:T(8,128)(2,1)S(1)} %get-tuple-element.24), channel_id=1, source_target_pairs={{0,7},{1,0},{2,1},{3,2},{4,3},{5,4},{6,5},{7,6},{8,15},{9,8},{10,9... | collective-permute-start | bytes 786440 | tf_op jit(solution)/shard_map/ppermute | solution.py:24
  182.6 2.5 %collective-permute-done.21 = bf16[64,2048]{1,0:T(8,128)(2,1)S(1)} collective-permute-done((bf16[64,2048]{1,0:T(8,128)(2,1)S(1)}, bf16[64,2048]{1,0:T(8,128)(2,1)S(1)}, u32[]{:S(2)}, u32[]{:S(2)}) %collective-permute-start.21) | collective-permute-done | bytes 262176 | tf_op jit(solution)/shard_map/ppermute | solution.py:24
  185.1 3.4 %collective-permute-done.18 = bf16[64,2048]{1,0:T(8,128)(2,1)S(1)} collective-permute-done((bf16[64,2048]{1,0:T(8,128)(2,1)S(1)}, bf16[64,2048]{1,0:T(8,128)(2,1)S(1)}, u32[]{:S(2)}, u32[]{:S(2)}) %collective-permute-start.18) | collective-permute-done | bytes 262176 | tf_op jit(solution)/shard_map/ppermute | solution.py:24
  188.5 2.8 %collective-permute-done.24 = bf16[64,2048]{1,0:T(8,128)(2,1)S(1)} collective-permute-done((bf16[64,2048]{1,0:T(8,128)(2,1)S(1)}, bf16[64,2048]{1,0:T(8,128)(2,1)S(1)}, u32[]{:S(2)}, u32[]{:S(2)}) %collective-permute-start.24) | collective-permute-done | bytes 262176 | tf_op jit(solution)/shard_map/ppermute | solution.py:24
  191.3 0.3 fusion.11
  191.6 0.8 pad_maximum_fusion
  (58 shorter events, 0.8 us)
Async XLA Ops:
  1.1 13.5 %collective-permute-start = (bf16[64,2048]{1,0:T(8,128)(2,1)S(1)}, bf16[64,2048]{1,0:T(8,128)(2,1)S(1)}, u32[]{:S(2)}, u32[]{:S(2)}) collective-permute-start(bf16[64,2048]{1,0:T(8,128)(2,1)S(1)} %get-tuple-element.38), channel_id=1, source_target_pairs={{0,1},{1,2},{2,3},{3,4},{4,5},{5,6},{6,7},{7,0},{8,9},{9,10},{10,1... | collective-permute-start | bytes 786440 | tf_op jit(solution)/shard_map/ppermute | solution.py:24
  3.1 18.9 %collective-permute-start.8 = (bf16[64,2048]{1,0:T(8,128)(2,1)S(1)}, bf16[64,2048]{1,0:T(8,128)(2,1)S(1)}, u32[]{:S(2)}, u32[]{:S(2)}) collective-permute-start(bf16[64,2048]{1,0:T(8,128)(2,1)S(1)} %get-tuple-element.38), channel_id=1, source_target_pairs={{0,7},{1,0},{2,1},{3,2},{4,3},{5,4},{6,5},{7,6},{8,15},{9,8},{10,9... | collective-permute-start | bytes 786440 | tf_op jit(solution)/shard_map/ppermute | solution.py:24
  7.1 11.2 %collective-permute-start.4 = (bf16[64,2048]{1,0:T(8,128)(2,1)S(1)}, bf16[64,2048]{1,0:T(8,128)(2,1)S(1)}, u32[]{:S(2)}, u32[]{:S(2)}) collective-permute-start(bf16[64,2048]{1,0:T(8,128)(2,1)S(1)} %get-tuple-element.37), channel_id=1, source_target_pairs={{0,7},{1,0},{2,1},{3,2},{4,3},{5,4},{6,5},{7,6},{8,15},{9,8},{10,9... | collective-permute-start | bytes 786440 | tf_op jit(solution)/shard_map/ppermute | solution.py:24
  9.0 13.4 %collective-permute-start.11 = (bf16[64,2048]{1,0:T(8,128)(2,1)S(1)}, bf16[64,2048]{1,0:T(8,128)(2,1)}, u32[]{:S(2)}, u32[]{:S(2)}) collective-permute-start(bf16[64,2048]{1,0:T(8,128)(2,1)S(1)} %get-tuple-element.37), channel_id=1, source_target_pairs={{0,1},{1,2},{2,3},{3,4},{4,5},{5,6},{6,7},{7,0},{8,9},{9,10},{10,1... | collective-permute-start | bytes 786440 | tf_op jit(solution)/shard_map/ppermute | solution.py:24
  9.9 20.9 %collective-permute-start.14 = (bf16[8,2048]{1,0:T(8,128)(2,1)S(1)}, bf16[8,2048]{1,0:T(8,128)(2,1)S(1)}, u32[]{:S(2)}, u32[]{:S(2)}) collective-permute-start(bf16[8,2048]{1,0:T(8,128)(2,1)S(1)} %slice.116), channel_id=1, source_target_pairs={{0,8},{8,16},{16,24},{24,32},{32,40},{40,48},{48,56},{56,64},{64,7... | collective-permute-start | bytes 98312 | tf_op jit(solution)/shard_map/ppermute | solution.py:29
  14.5 41.3 %collective-permute-start.1 = (bf16[64,2048]{1,0:T(8,128)(2,1)S(1)}, bf16[64,2048]{1,0:T(8,128)(2,1)}, u32[]{:S(2)}, u32[]{:S(2)}) collective-permute-start(bf16[64,2048]{1,0:T(8,128)(2,1)S(1)} %collective-permute-done.refs_2_), channel_id=1, source_target_pairs={{0,1},{1,2},{2,3},{3,4},{4,5},{5,6},{6,7},{7,0},{8,9},{9,10},{10,1... | collective-permute-start | bytes 786440 | tf_op jit(solution)/shard_map/ppermute | solution.py:24
  18.3 38.3 %collective-permute-start.5 = (bf16[64,2048]{1,0:T(8,128)(2,1)S(1)}, bf16[64,2048]{1,0:T(8,128)(2,1)}, u32[]{:S(2)}, u32[]{:S(2)}) collective-permute-start(bf16[64,2048]{1,0:T(8,128)(2,1)S(1)} %collective-permute-done.4.refs_1_), channel_id=1, source_target_pairs={{0,7},{1,0},{2,1},{3,2},{4,3},{5,4},{6,5},{7,6},{8,15},{9,8},{10,9... | collective-permute-start | bytes 786440 | tf_op jit(solution)/shard_map/ppermute | solution.py:24
  22.0 37.1 %collective-permute-start.9 = (bf16[64,2048]{1,0:T(8,128)(2,1)S(1)}, bf16[64,2048]{1,0:T(8,128)(2,1)}, u32[]{:S(2)}, u32[]{:S(2)}) collective-permute-start(bf16[64,2048]{1,0:T(8,128)(2,1)S(1)} %collective-permute-done.8.refs_0_), channel_id=1, source_target_pairs={{0,7},{1,0},{2,1},{3,2},{4,3},{5,4},{6,5},{7,6},{8,15},{9,8},{10,9... | collective-permute-start | bytes 786440 | tf_op jit(solution)/shard_map/ppermute | solution.py:24
  22.4 37.1 %collective-permute-start.12 = (bf16[64,2048]{1,0:T(8,128)(2,1)}, bf16[64,2048]{1,0:T(8,128)(2,1)}, u32[]{:S(2)}, u32[]{:S(2)}) collective-permute-start(bf16[64,2048]{1,0:T(8,128)(2,1)} %collective-permute-done.11.refs_3_), channel_id=1, source_target_pairs={{0,1},{1,2},{2,3},{3,4},{4,5},{5,6},{6,7},{7,0},{8,9},{9,10},{10,1... | collective-permute-start | bytes 786440 | tf_op jit(solution)/shard_map/ppermute | solution.py:24
  24.7 1.0 copy-start.5
  25.7 35.4 %copy-start.6 = (bf16[2048,1,1288]{0,2,1:T(8,128)(2,1)S(1)}, bf16[2048,1,1288]{0,2,1:T(8,128)(2,1)}, u32[]{:S(2)}) copy-start(bf16[2048,1,1288]{0,2,1:T(8,128)(2,1)} %param.13) | copy-start | bytes 15826948
  55.8 8.7 %collective-permute-start.2 = (bf16[64,2048]{1,0:T(8,128)(2,1)}, bf16[64,2048]{1,0:T(8,128)(2,1)}, u32[]{:S(2)}, u32[]{:S(2)}) collective-permute-start(bf16[64,2048]{1,0:T(8,128)(2,1)} %collective-permute-done.1.refs_2_), channel_id=1, source_target_pairs={{0,1},{1,2},{2,3},{3,4},{4,5},{5,6},{6,7},{7,0},{8,9},{9,10},{10,1... | collective-permute-start | bytes 786440 | tf_op jit(solution)/shard_map/ppermute | solution.py:24
  56.6 8.0 %collective-permute-start.6 = (bf16[64,2048]{1,0:T(8,128)(2,1)}, bf16[64,2048]{1,0:T(8,128)(2,1)}, u32[]{:S(2)}, u32[]{:S(2)}) collective-permute-start(bf16[64,2048]{1,0:T(8,128)(2,1)} %collective-permute-done.5.refs_1_), channel_id=1, source_target_pairs={{0,7},{1,0},{2,1},{3,2},{4,3},{5,4},{6,5},{7,6},{8,15},{9,8},{10,9... | collective-permute-start | bytes 786440 | tf_op jit(solution)/shard_map/ppermute | solution.py:24
  59.0 18.5 %collective-permute-start.10 = (bf16[64,2048]{1,0:T(8,128)(2,1)}, bf16[64,2048]{1,0:T(8,128)(2,1)}, u32[]{:S(2)}, u32[]{:S(2)}) collective-permute-start(bf16[64,2048]{1,0:T(8,128)(2,1)} %collective-permute-done.9.refs_0_), channel_id=1, source_target_pairs={{0,7},{1,0},{2,1},{3,2},{4,3},{5,4},{6,5},{7,6},{8,15},{9,8},{10,9... | collective-permute-start | bytes 786440 | tf_op jit(solution)/shard_map/ppermute | solution.py:24
  59.5 18.0 %collective-permute-start.13 = (bf16[64,2048]{1,0:T(8,128)(2,1)}, bf16[64,2048]{1,0:T(8,128)(2,1)}, u32[]{:S(2)}, u32[]{:S(2)}) collective-permute-start(bf16[64,2048]{1,0:T(8,128)(2,1)} %collective-permute-done.12.refs_3_), channel_id=1, source_target_pairs={{0,1},{1,2},{2,3},{3,4},{4,5},{5,6},{6,7},{7,0},{8,9},{9,10},{10,1... | collective-permute-start | bytes 786440 | tf_op jit(solution)/shard_map/ppermute | solution.py:24
  64.5 18.0 %collective-permute-start.3 = (bf16[64,2048]{1,0:T(8,128)(2,1)}, bf16[64,2048]{1,0:T(8,128)(2,1)S(1)}, u32[]{:S(2)}, u32[]{:S(2)}) collective-permute-start(bf16[64,2048]{1,0:T(8,128)(2,1)} %collective-permute-done.2.refs_2_), channel_id=1, source_target_pairs={{0,1},{1,2},{2,3},{3,4},{4,5},{5,6},{6,7},{7,0},{8,9},{9,10},{10,1... | collective-permute-start | bytes 786440 | tf_op jit(solution)/shard_map/ppermute | solution.py:24
  64.5 18.0 %collective-permute-start.7 = (bf16[64,2048]{1,0:T(8,128)(2,1)}, bf16[64,2048]{1,0:T(8,128)(2,1)S(1)}, u32[]{:S(2)}, u32[]{:S(2)}) collective-permute-start(bf16[64,2048]{1,0:T(8,128)(2,1)} %collective-permute-done.6.refs_1_), channel_id=1, source_target_pairs={{0,7},{1,0},{2,1},{3,2},{4,3},{5,4},{6,5},{7,6},{8,15},{9,8},{10,9... | collective-permute-start | bytes 786440 | tf_op jit(solution)/shard_map/ppermute | solution.py:24
  87.2 1.5 copy-start
  89.4 32.6 %copy-start.11 = (s32[3]{0:T(128)S(1)}, s32[3]{0:T(128)}, u32[]{:S(2)}) copy-start(s32[3]{0:T(128)} %constant.47.clone) | copy-start | bytes 40
  89.4 32.6 %copy-start.9 = (f32[8]{0:T(128)S(1)}, f32[8]{0:T(128)}, u32[]{:S(2)}) copy-start(f32[8]{0:T(128)} %param.18) | copy-start | bytes 100
  98.6 1.3 copy-start.1
  116.8 15.0 %copy-start.8 = (f32[512]{0:T(512)S(1)}, f32[512]{0:T(512)}, u32[]{:S(2)}) copy-start(f32[512]{0:T(512)} %param.19) | copy-start | bytes 6148
  116.8 15.0 %all-to-all-start.1 = ((bf16[32,16,128]{2,1,0:T(8,128)(2,1)}), bf16[32,16,128]{2,1,0:T(8,128)(2,1)S(1)}, u32[]{:S(2)}, u32[]{:S(2)}) async-start(bf16[32,16,128]{2,1,0:T(8,128)(2,1)} %prefix.1), calls=%async_computation.1 | async-start | bytes 262144 | tf_op jit(solution)/shard_map/all_to_all | solution.py:437
  129.1 1.4 copy-start.2
  130.5 1.3 copy-start.4
  132.0 1.6 copy-start.3
  138.5 14.1 %copy-start.10 = (s32[5]{0:T(128)S(1)}, s32[5]{0:T(128)}, u32[]{:S(2)}) copy-start(s32[5]{0:T(128)} %constant.48.clone) | copy-start | bytes 64
  138.6 10.4 %collective-permute-start.15 = (bf16[64,2048]{1,0:T(8,128)(2,1)S(1)}, bf16[64,2048]{1,0:T(8,128)(2,1)S(1)}, u32[]{:S(2)}, u32[]{:S(2)}) collective-permute-start(bf16[64,2048]{1,0:T(8,128)(2,1)S(1)} %get-tuple-element.33), channel_id=1, source_target_pairs={{0,1},{1,2},{2,3},{3,4},{4,5},{5,6},{6,7},{7,0},{8,9},{9,10},{10,1... | collective-permute-start | bytes 786440 | tf_op jit(solution)/shard_map/ppermute | solution.py:24
  138.7 10.3 %collective-permute-start.25 = (bf16[64,2048]{1,0:T(8,128)(2,1)S(1)}, bf16[64,2048]{1,0:T(8,128)(2,1)S(1)}, u32[]{:S(2)}, u32[]{:S(2)}) collective-permute-start(bf16[64,2048]{1,0:T(8,128)(2,1)S(1)} %get-tuple-element.34), channel_id=1, source_target_pairs={{0,7},{1,0},{2,1},{3,2},{4,3},{5,4},{6,5},{7,6},{8,15},{9,8},{10,9... | collective-permute-start | bytes 786440 | tf_op jit(solution)/shard_map/ppermute | solution.py:24
  141.9 18.5 %collective-permute-start.22 = (bf16[64,2048]{1,0:T(8,128)(2,1)S(1)}, bf16[64,2048]{1,0:T(8,128)(2,1)S(1)}, u32[]{:S(2)}, u32[]{:S(2)}) collective-permute-start(bf16[64,2048]{1,0:T(8,128)(2,1)S(1)} %get-tuple-element.35), channel_id=1, source_target_pairs={{0,1},{1,2},{2,3},{3,4},{4,5},{5,6},{6,7},{7,0},{8,9},{9,10},{10,1... | collective-permute-start | bytes 786440 | tf_op jit(solution)/shard_map/ppermute | solution.py:24
  141.9 18.5 %collective-permute-start.19 = (bf16[64,2048]{1,0:T(8,128)(2,1)S(1)}, bf16[64,2048]{1,0:T(8,128)(2,1)S(1)}, u32[]{:S(2)}, u32[]{:S(2)}) collective-permute-start(bf16[64,2048]{1,0:T(8,128)(2,1)S(1)} %get-tuple-element.36), channel_id=1, source_target_pairs={{0,7},{1,0},{2,1},{3,2},{4,3},{5,4},{6,5},{7,6},{8,15},{9,8},{10,9... | collective-permute-start | bytes 786440 | tf_op jit(solution)/shard_map/ppermute | solution.py:24
  149.2 11.2 %collective-permute-start.16 = (bf16[64,2048]{1,0:T(8,128)(2,1)S(1)}, bf16[64,2048]{1,0:T(8,128)(2,1)S(1)}, u32[]{:S(2)}, u32[]{:S(2)}) collective-permute-start(bf16[64,2048]{1,0:T(8,128)(2,1)S(1)} %get-tuple-element.31), channel_id=1, source_target_pairs={{0,1},{1,2},{2,3},{3,4},{4,5},{5,6},{6,7},{7,0},{8,9},{9,10},{10,1... | collective-permute-start | bytes 786440 | tf_op jit(solution)/shard_map/ppermute | solution.py:24
  149.3 11.1 %collective-permute-start.26 = (bf16[64,2048]{1,0:T(8,128)(2,1)S(1)}, bf16[64,2048]{1,0:T(8,128)(2,1)S(1)}, u32[]{:S(2)}, u32[]{:S(2)}) collective-permute-start(bf16[64,2048]{1,0:T(8,128)(2,1)S(1)} %get-tuple-element.32), channel_id=1, source_target_pairs={{0,7},{1,0},{2,1},{3,2},{4,3},{5,4},{6,5},{7,6},{8,15},{9,8},{10,9... | collective-permute-start | bytes 786440 | tf_op jit(solution)/shard_map/ppermute | solution.py:24
  160.4 15.5 %copy-start.7 = (bf16[5,128,2048]{2,1,0:T(8,128)(2,1)S(1)}, bf16[5,128,2048]{2,1,0:T(8,128)(2,1)}, u32[]{:S(2)}) copy-start(bf16[5,128,2048]{2,1,0:T(8,128)(2,1)} %finish.3) | copy-start | bytes 7864324
  162.1 10.8 %collective-permute-start.17 = (bf16[64,2048]{1,0:T(8,128)(2,1)S(1)}, bf16[64,2048]{1,0:T(8,128)(2,1)S(1)}, u32[]{:S(2)}, u32[]{:S(2)}) collective-permute-start(bf16[64,2048]{1,0:T(8,128)(2,1)S(1)} %get-tuple-element.27), channel_id=1, source_target_pairs={{0,1},{1,2},{2,3},{3,4},{4,5},{5,6},{6,7},{7,0},{8,9},{9,10},{10,1... | collective-permute-start | bytes 786440 | tf_op jit(solution)/shard_map/ppermute | solution.py:24
  162.4 10.4 %collective-permute-start.27 = (bf16[64,2048]{1,0:T(8,128)(2,1)S(1)}, bf16[64,2048]{1,0:T(8,128)(2,1)S(1)}, u32[]{:S(2)}, u32[]{:S(2)}) collective-permute-start(bf16[64,2048]{1,0:T(8,128)(2,1)S(1)} %get-tuple-element.28), channel_id=1, source_target_pairs={{0,7},{1,0},{2,1},{3,2},{4,3},{5,4},{6,5},{7,6},{8,15},{9,8},{10,9... | collective-permute-start | bytes 786440 | tf_op jit(solution)/shard_map/ppermute | solution.py:24
  165.6 10.2 %collective-permute-start.23 = (bf16[64,2048]{1,0:T(8,128)(2,1)S(1)}, bf16[64,2048]{1,0:T(8,128)(2,1)S(1)}, u32[]{:S(2)}, u32[]{:S(2)}) collective-permute-start(bf16[64,2048]{1,0:T(8,128)(2,1)S(1)} %get-tuple-element.29), channel_id=1, source_target_pairs={{0,1},{1,2},{2,3},{3,4},{4,5},{5,6},{6,7},{7,0},{8,9},{9,10},{10,1... | collective-permute-start | bytes 786440 | tf_op jit(solution)/shard_map/ppermute | solution.py:24
  165.6 10.2 %collective-permute-start.20 = (bf16[64,2048]{1,0:T(8,128)(2,1)S(1)}, bf16[64,2048]{1,0:T(8,128)(2,1)S(1)}, u32[]{:S(2)}, u32[]{:S(2)}) collective-permute-start(bf16[64,2048]{1,0:T(8,128)(2,1)S(1)} %get-tuple-element.30), channel_id=1, source_target_pairs={{0,7},{1,0},{2,1},{3,2},{4,3},{5,4},{6,5},{7,6},{8,15},{9,8},{10,9... | collective-permute-start | bytes 786440 | tf_op jit(solution)/shard_map/ppermute | solution.py:24
  176.3 8.8 %collective-permute-start.21 = (bf16[64,2048]{1,0:T(8,128)(2,1)S(1)}, bf16[64,2048]{1,0:T(8,128)(2,1)S(1)}, u32[]{:S(2)}, u32[]{:S(2)}) collective-permute-start(bf16[64,2048]{1,0:T(8,128)(2,1)S(1)} %get-tuple-element.26), channel_id=1, source_target_pairs={{0,7},{1,0},{2,1},{3,2},{4,3},{5,4},{6,5},{7,6},{8,15},{9,8},{10,9... | collective-permute-start | bytes 786440 | tf_op jit(solution)/shard_map/ppermute | solution.py:24
  179.3 9.2 %collective-permute-start.18 = (bf16[64,2048]{1,0:T(8,128)(2,1)S(1)}, bf16[64,2048]{1,0:T(8,128)(2,1)S(1)}, u32[]{:S(2)}, u32[]{:S(2)}) collective-permute-start(bf16[64,2048]{1,0:T(8,128)(2,1)S(1)} %get-tuple-element.23), channel_id=1, source_target_pairs={{0,1},{1,2},{2,3},{3,4},{4,5},{5,6},{6,7},{7,0},{8,9},{9,10},{10,1... | collective-permute-start | bytes 786440 | tf_op jit(solution)/shard_map/ppermute | solution.py:24
  179.3 9.2 %collective-permute-start.28 = (bf16[64,2048]{1,0:T(8,128)(2,1)S(1)}, bf16[64,2048]{1,0:T(8,128)(2,1)S(1)}, u32[]{:S(2)}, u32[]{:S(2)}) collective-permute-start(bf16[64,2048]{1,0:T(8,128)(2,1)S(1)} %get-tuple-element.24), channel_id=1, source_target_pairs={{0,7},{1,0},{2,1},{3,2},{4,3},{5,4},{6,5},{7,6},{8,15},{9,8},{10,9... | collective-permute-start | bytes 786440 | tf_op jit(solution)/shard_map/ppermute | solution.py:24
  182.6 8.8 %collective-permute-start.24 = (bf16[64,2048]{1,0:T(8,128)(2,1)S(1)}, bf16[64,2048]{1,0:T(8,128)(2,1)S(1)}, u32[]{:S(2)}, u32[]{:S(2)}) collective-permute-start(bf16[64,2048]{1,0:T(8,128)(2,1)S(1)} %get-tuple-element.25), channel_id=1, source_target_pairs={{0,1},{1,2},{2,3},{3,4},{4,5},{5,6},{6,7},{7,0},{8,9},{9,10},{10,1... | collective-permute-start | bytes 786440 | tf_op jit(solution)/shard_map/ppermute | solution.py:24
